TPU v7x, 768 devices: a whole 4x8x12 slice. The times are simulated.
768 devices in a mesh: pts: 96 (over y, z), grp: 8 (over x, core).
Axes of the slice: x: 4, y: 8, z: 12, core: 2. Of those that a mesh axis runs over, the one named last changes fastest.
Arguments:
- points: bfloat16 [786432, 1024], P(('pts', 'grp')), may hold values from -24 to 24
- send_counts: int32 [768, 8], P(('pts', 'grp')), may hold values from 16 to 128, as said below
- assign_one: int32 [786432], P(('pts', 'grp')), may hold values from 0 to 127, as said below
- parent_two: int32 [98304], P(('pts', 'grp')), may hold values from 0 to 255, as said below
- parent_three: int32 [256], replicated, may hold values from 0 to 31, as said below
- parent_four: int32 [32], replicated, may hold values from 0 to 7, as said below
Outputs:
- centroids_one: float32 [98304, 1024], P(('pts', 'grp'))
- centroids_two: float32 [256, 1024], replicated
- centroids_three: float32 [32, 1024], replicated
- centroids_four: float32 [8, 1024], replicated
Inputs may be any that keep to these rules, and one draw needn't show every extreme that they name: `send_counts`: blocks are filled from their first slot; for each pts index one block index, drawn from the seed, is full (128) on every device of that pts index. `assign_one`: every level-1 centroid is named by at least one live slot. `parent_two`: every level-2 centroid has at least one child. `parent_three`: every level-3 centroid has at least one child. `parent_four`: every level-4 centroid has at least one child.
All inputs are finite; a program needn't handle non-finite values.
Results may differ from a plain program's by a relative error of at most 0.0003.
Values may be sent and summed in bfloat16 or wider, within the bound.
No kernel may reach another device: no remote copies, remote signals or barrier semaphores. Data moves between devices by JAX's collectives and lax.ppermute only.
A program may use at most 32 MiB of HBM per device.

v0:
```python
import jax
import jax.numpy as jnp
from jax import lax
from jax.sharding import PartitionSpec as P

K2 = 256
K3 = 32
K4 = 8


def member_sums(onehot, rows, precision):
    return lax.dot_general(
        onehot,
        rows,
        (((0,), (0,)), ((), ())),
        precision=precision,
        preferred_element_type=jnp.float32,
    )


def coarse_mean(rows, parents, count):
    onehot = (parents[:, None] == jnp.arange(count, dtype=jnp.int32)[None, :]).astype(jnp.float32)
    sums = member_sums(onehot, rows, lax.Precision.HIGHEST)
    return sums / jnp.sum(onehot, axis=0)[:, None]


def local(points, send_counts, assign_one, parent_two, parent_three, parent_four):
    groups = lax.axis_size("grp")
    slots = points.shape[0]
    cap = slots // groups
    kdev = parent_two.shape[0]
    within = jnp.arange(slots, dtype=jnp.int32) % cap
    arrived, idents, counts = (
        lax.all_to_all(points, "grp", split_axis=0, concat_axis=0, tiled=True),
        lax.all_to_all(assign_one, "grp", split_axis=0, concat_axis=0, tiled=True),
        lax.all_to_all(send_counts[0], "grp", split_axis=0, concat_axis=0, tiled=True),
    )
    live = within < jnp.repeat(counts, cap)
    onehot = (
        (idents[:, None] == jnp.arange(kdev, dtype=jnp.int32)[None, :]) & live[:, None]
    ).astype(jnp.bfloat16)
    sums_one = member_sums(onehot, arrived, None)
    count_one = jnp.sum(onehot.astype(jnp.float32), axis=0)
    centroids_one = sums_one / count_one[:, None]
    onehot_two = (parent_two[:, None] == jnp.arange(K2, dtype=jnp.int32)[None, :]).astype(
        jnp.float32
    )
    partial_two = member_sums(onehot_two, centroids_one, lax.Precision.HIGHEST)
    sums_two, count_two = lax.psum((partial_two, jnp.sum(onehot_two, axis=0)), ("pts", "grp"))
    centroids_two = sums_two / count_two[:, None]
    centroids_three = coarse_mean(centroids_two, parent_three, K3)
    centroids_four = coarse_mean(centroids_three, parent_four, K4)
    return (centroids_one, centroids_two, centroids_three, centroids_four)


def solution(mesh):
    placed = (
        P(("pts", "grp"), None),
        P(("pts", "grp"), None),
        P(("pts", "grp")),
        P(("pts", "grp")),
        P(),
        P(),
    )
    return jax.shard_map(
        local,
        mesh=mesh,
        in_specs=placed,
        out_specs=(P(("pts", "grp"), None), P(), P(), P()),
        check_vma=False,
    )
```

profile of v0, /device:TPU:1, one launch (start us, length us, event | category | flops | bytes accessed | tf_op | source)
XLA Modules:
  0.0 541.2 jit_solution(11456993128414346947)
XLA Ops:
  7.2 0.7 copy.15
  7.9 17.4 %all_to_all.33 = s32[8,1,1]{2,1,0:T(1,128)S(1)} all-to-all(s32[8,1,1]{2,1,0:T(1,128)S(1)} %copy.15), channel_id=1, replica_groups=mesh['pts'=96,'grp'=8] {'grp'}, dimensions={0} | all-to-all | bytes 64 | tf_op jit(solution)/shard_map/all_to_all | solution.py:36
  25.3 8.4 %all_to_all.34 = s32[8,128,1]{1,2,0:T(1,128)S(1)} all-to-all(s32[8,128,1]{1,2,0:T(1,128)} %bitcast.17), channel_id=1, replica_groups=mesh['pts'=96,'grp'=8] {'grp'}, dimensions={0} | all-to-all | bytes 8192 | tf_op jit(solution)/shard_map/all_to_all | solution.py:35
  33.7 4.2 all-to-all-start.2
  37.9 0.0 copy-start.4
  37.9 0.0 all-reduce.2.cloned.1.call-start
  37.9 0.2 reduce
  38.2 0.1 fusion.8
  38.2 0.4 convert_reduce_fusion
  38.6 25.7 %all-to-all-done.2 = bf16[8,128,1024]{2,1,0:T(8,128)(2,1)S(1)} async-done(((bf16[8,128,1024]{2,1,0:T(8,128)(2,1)}), bf16[8,128,1024]{2,1,0:T(8,128)(2,1)S(1)}, u32[]{:S(2)}, u32[]{:S(2)}) %all-to-all-start.2) | async-done | bytes 2097184 | tf_op jit(solution)/shard_map/all_to_all | solution.py:34
  64.3 0.8 convolution_divide_fusion
  65.1 0.0 copy-done.4
  65.1 0.0 copy-start.2
  65.1 0.0 copy-start.5
  65.1 0.0 copy-start.3
  65.1 1.7 fusion.5
  66.8 0.0 all-reduce.2.cloned.1.call-update
  66.8 0.1 convert_reduce_fusion.1
  66.9 112.1 %psum.15 = f32[256]{0:T(256)S(1)} all-reduce(f32[256]{0:T(256)S(1)} %convert_reduce_fusion.1), channel_id=1, replica_groups=mesh['pts'=96,'grp'=8] {'pts','grp'}, use_global_device_ids=true, to_apply=%region_3.4 | all-reduce | flops 256 | bytes 2048 | tf_op jit(solution)/shard_map/psum | solution.py:49
  179.0 0.0 copy-done.5
  179.0 0.1 convert_reduce_fusion.3
  179.2 0.0 copy-done.3
  179.2 0.1 convert_reduce_fusion.2
  179.3 352.4 %all-reduce.2.cloned.1.call-done = f32[256,1024]{1,0:T(8,128)} async-done(((f32[256,1024]{1,0:T(8,128)}), f32[256,1024]{1,0:T(8,128)}) %all-reduce.2.cloned.1.call-update) | async-done | bytes 1048592 | tf_op jit(solution)/shard_map/psum | solution.py:49
  531.7 1.4 broadcast_divide_fusion
  533.0 0.0 copy-done.2
  533.1 0.0 copy-start
  533.1 0.5 convolution_divide_fusion.1
  533.6 0.0 copy-start.1
  533.6 0.8 convolution_divide_fusion.2
  534.3 0.0 copy-done
  534.4 0.0 copy-done.1
Async XLA Ops:
  33.7 30.6 %all-to-all-start.2 = ((bf16[8,128,1024]{2,1,0:T(8,128)(2,1)}), bf16[8,128,1024]{2,1,0:T(8,128)(2,1)S(1)}, u32[]{:S(2)}, u32[]{:S(2)}) async-start(bf16[8,128,1024]{2,1,0:T(8,128)(2,1)} %bitcast.13), calls=%async_computation.2 | async-start | bytes 4194304 | tf_op jit(solution)/shard_map/all_to_all | solution.py:34
  37.9 27.2 %copy-start.4 = (s32[128]{0:T(128)S(1)}, s32[128]{0:T(128)}, u32[]{:S(2)}) copy-start(s32[128]{0:T(128)} %param.9) | copy-start | bytes 1540
  37.9 493.7 %all-reduce.2.cloned.1.call-start = ((), (), s32[]{:S(2)}) async-start(), calls=%async_computation.3 | async-start | bytes 2097152 | tf_op jit(solution)/shard_map/psum | solution.py:49
  65.1 467.9 %copy-start.2 = (f32[128,1024]{1,0:T(8,128)}, f32[128,1024]{1,0:T(8,128)S(1)}, u32[]{:S(2)}) copy-start(f32[128,1024]{1,0:T(8,128)S(1)} %convolution_divide_fusion) | copy-start | bytes 1572868
  65.1 113.9 %copy-start.5 = (s32[32]{0:T(128)S(1)}, s32[32]{0:T(128)}, u32[]{:S(2)}) copy-start(s32[32]{0:T(128)} %param.11) | copy-start | bytes 388
  65.1 114.0 %copy-start.3 = (s32[256]{0:T(256)S(1)}, s32[256]{0:T(256)}, u32[]{:S(2)}) copy-start(s32[256]{0:T(256)} %param.10) | copy-start | bytes 3076
  533.1 1.3 copy-start
  533.6 0.8 copy-start.1
Sparse Core Ops, SparseCore 0:
  67.0 464.6 all-reduce.1
where the time goes:
time: 543 us; the launch traced here: 541 us
  waiting for transfers between devices  378 us (70%)
  blocking collectives  138 us (25%)
  between operations  14.1 us (3%)
    psum x1, waiting for transfers between devices, local(): lax.psum((partial_two, jnp.sum(onehot_two, axis=0)), ('pts', 'grp'))  352 us
    psum x1, blocking collectives, local(): lax.psum((partial_two, jnp.sum(onehot_two, axis=0)), ('pts', 'grp'))  112 us
    all_to_all x1, waiting for transfers between devices, local(): lax.all_to_all(points, 'grp', split_axis=0, concat_axis=0, tiled=True)  25.7 us
    all_to_all x1, blocking collectives, local(): lax.all_to_all(send_counts[0], 'grp', split_axis=0, concat_axis=0, tiled=...  17.4 us
  transfers between devices with their start and end apart: 2, of which 2 were waited for; matrix products, arithmetic and copies ran while one was open for 0% of the time, Pallas kernels for 0%

commit v1 on v0

v1 whole, which is shorter than its diff:
```python
import jax
import jax.numpy as jnp
from jax import lax
from jax.sharding import Mesh, PartitionSpec as P

K2 = 256
K3 = 32
K4 = 8
F32 = jnp.float32
BF16 = jnp.bfloat16


def dot(a, b, dims, precision=None):
    return lax.dot_general(a, b, (dims, ((), ())), precision=precision, preferred_element_type=F32)


def split_three(w):
    hi = lax.reduce_precision(w, 8, 7)
    rest = w - hi
    mid = lax.reduce_precision(rest, 8, 7)
    return hi, mid, rest - mid


def coarse_mean(rows, parents, count):
    onehot = (parents[None, :] == jnp.arange(count, dtype=jnp.int32)[:, None]).astype(F32)
    sums = dot(onehot, rows, ((1,), (0,)), lax.Precision.HIGHEST)
    return sums / jnp.sum(onehot, axis=1)[:, None]


def gather(rows, axes, n):
    wide = jnp.broadcast_to(rows[None], (n,) + rows.shape)
    return lax.all_to_all(wide, axes, split_axis=0, concat_axis=0, tiled=True)


def local(points, send_counts, assign_one, parent_two, parent_three, parent_four):
    nx, nc, npts = lax.axis_size("x"), lax.axis_size("c"), lax.axis_size("pts")
    groups = nx * nc
    slots, depth = points.shape
    cap = slots // groups
    kdev = parent_two.shape[0]
    half = depth // nc
    cols = half // nx
    x, c = lax.axis_index("x"), lax.axis_index("c")

    mine = lax.dynamic_slice_in_dim(points, c * half, half, 1)
    theirs = lax.ppermute(
        lax.dynamic_slice_in_dim(points, (1 - c) * half, half, 1), "c", [(0, 1), (1, 0)]
    )

    within = lax.broadcasted_iota(jnp.int32, (groups, cap), 1)
    idents = jnp.where(
        within < send_counts.reshape(groups, 1), assign_one.reshape(groups, cap), -1
    )
    pad = jnp.zeros((16 - groups - 1, cap), jnp.int32)
    known = gather(jnp.concatenate([idents, parent_two[None], pad]), ("x", "c"), groups)
    ids = known[:, :groups]
    parents = known[:, groups]

    ks = jnp.arange(kdev, dtype=jnp.int32)
    count_one = jnp.sum((ids[:, :, None, :] == ks[None, None, :, None]).astype(F32), axis=(0, 3))
    inverse = 1.0 / count_one
    child = jnp.sum(
        (parents.reshape(1, -1) == jnp.arange(K2, dtype=jnp.int32)[:, None]).astype(F32), axis=1
    )

    partial = 0.0
    for core, rows in ((c, mine), (1 - c, theirs)):
        own = lax.dynamic_index_in_dim(ids, x * nc + core, 0, keepdims=False)
        hit = own[:, None, :] == ks[None, :, None]
        weight = jnp.sum(jnp.where(hit, inverse[:, :, None], 0.0), axis=1).reshape(slots)
        key = jnp.sum(jnp.where(hit, parents[:, :, None] + 1, 0), axis=1).reshape(slots) - 1
        chosen = key[None, :] == jnp.arange(K2, dtype=jnp.int32)[:, None]
        for part in split_three(weight):
            onehot = jnp.where(chosen, part[None, :], 0.0).astype(BF16)
            partial = partial + dot(onehot, rows, ((1,), (0,)))
    partial = partial.reshape(K2, nx, cols).transpose(1, 0, 2)
    sums = jnp.sum(
        lax.all_to_all(partial, "x", split_axis=0, concat_axis=0, tiled=True), axis=0
    )
    r = -(-K2 // npts)
    extra = r * npts - K2
    sums = jnp.pad(sums, ((0, extra), (0, 0))).reshape(npts, r, cols)
    child = jnp.pad(jnp.pad(child, (0, extra)).reshape(npts, 1, r), ((0, 0), (0, 0), (0, cols - r)))
    both = lax.all_to_all(
        jnp.concatenate([sums, child], axis=1), "pts", split_axis=0, concat_axis=0, tiled=True
    )
    both = jnp.sum(both, axis=0)
    cent = both[:r] / both[r, :r][:, None]
    two = gather(cent, "pts", npts).reshape(npts * r, cols)[:K2]
    three = coarse_mean(two, parent_three, K3)
    four = coarse_mean(three, parent_four, K4)
    upper = gather(jnp.concatenate([two, three, four]), ("x", "c"), groups)
    upper = upper.reshape(nx, nc, K2 + K3 + K4, cols).transpose(2, 1, 0, 3)
    upper = upper.reshape(K2 + K3 + K4, depth)

    blocks = [v.reshape(nx, nc, cap, half) for v in (mine, theirs)]
    sums_one = [0.0] * nc
    for k in range(nx):
        to = lax.rem(x + k, nx)
        sent = jnp.stack([lax.dynamic_index_in_dim(v, to, 0, keepdims=False) for v in blocks])
        if k > 0:
            sent = lax.ppermute(sent, "x", [(j, (j + k) % nx) for j in range(nx)])
        source = lax.rem(x + nx - k, nx)
        for which, core in ((0, c), (1, 1 - c)):
            from_ids = lax.dynamic_index_in_dim(ids, source * nc + core, 0, keepdims=False)
            for o in range(nc):
                to_ids = lax.dynamic_index_in_dim(from_ids, x * nc + o, 0, keepdims=False)
                onehot = (to_ids[None, :] == ks[:, None]).astype(BF16)
                sums_one[o] = sums_one[o] + dot(onehot, sent[which, o], ((1,), (0,)))
    one = jnp.stack(sums_one) / lax.dynamic_slice_in_dim(count_one, x * nc, nc, 0)[:, :, None]
    kept = lax.dynamic_index_in_dim(one, c, 0, keepdims=False)
    given = lax.ppermute(
        lax.dynamic_index_in_dim(one, 1 - c, 0, keepdims=False), "c", [(0, 1), (1, 0)]
    )
    one = jnp.where(
        c == 0, jnp.concatenate([kept, given], 1), jnp.concatenate([given, kept], 1)
    )
    return one, upper[:K2], upper[K2 : K2 + K3], upper[K2 + K3 :]


def solution(mesh):
    npts, groups = mesh.devices.shape
    fine = Mesh(mesh.devices.reshape(npts, groups // 2, 2), ("pts", "x", "c"))
    every = ("pts", "x", "c")
    placed = (P(every, None), P(every, None), P(every), P(every), P(), P())
    return jax.shard_map(
        local,
        mesh=fine,
        in_specs=placed,
        out_specs=(P(every, None), P(), P(), P()),
        check_vma=False,
    )
```

time: 543 us -> 134 us (0.25)
  waiting for transfers between devices: 378 us -> 27.8 us
  blocking collectives: 138 us -> 0 us
  starting transfers between devices: 4.2 us -> 68.3 us
  matrix products: 3.74 us -> 18.6 us
  between operations: 14.1 us -> 1.28 us
  local copies, waits for them, and re-layouts: 0.77 us -> 9.65 us
  other arithmetic: 2.36 us -> 7.88 us
    psum x1 -> x0, waiting for transfers between devices: 352 us -> none  [local(): lax.psum((partial_two, jnp.sum(onehot_two, axis=0)), ('pts', 'grp'))]
    psum x1 -> x0, blocking collectives: 112 us -> none  [local(): lax.psum((partial_two, jnp.sum(onehot_two, axis=0)), ('pts', 'grp'))]
    all_to_all x1 -> x5, starting transfers between devices: 4.2 us -> 54.2 us  [the longest x3 35.9 us: gather(): return lax.all_to_all(wide, axes, split_axis=0, concat_axis=0, tiled=True)]
    all_to_all x2 -> x0, blocking collectives: 25.8 us -> none  [the longest x1 17.4 us: local(): lax.all_to_all(send_counts[0], 'grp', split_axis=0, concat_axis=0, tiled=...]
    dot_general x4 -> x24, matrix products: 3.74 us -> 18.6 us  [dot(): lax.dot_general(a, b, (dims, ((), ())), precision=precision, preferred_el...]
    ppermute x0 -> x5, starting transfers between devices: none -> 14.1 us  [the longest x3 10.1 us: local(): sent = lax.ppermute(sent, 'x', [(j, (j + k) % nx) for j in range(nx)])]
    all_to_all x1 -> x5, waiting for transfers between devices: 25.7 us -> 26.3 us  [the longest x3 22.2 us: gather(): return lax.all_to_all(wide, axes, split_axis=0, concat_axis=0, tiled=True)]
  transfers between devices with their start and end apart: 2 -> 10, of which waited for: 2 -> 4; matrix products, arithmetic and copies ran while one was open for 0% -> 20% of each run, Pallas kernels for 0% -> 0%
where the time goes in v1:
time: 134 us; the launch traced here: 133 us
  starting transfers between devices  68.3 us (51%)
  waiting for transfers between devices  27.8 us (21%)
  matrix products  18.6 us (14%)
  local copies, waits for them, and re-layouts  9.65 us (7%)
  other arithmetic  7.88 us (6%)
    all_to_all x3, starting transfers between devices, gather(): return lax.all_to_all(wide, axes, split_axis=0, concat_axis=0, tiled=True)  35.9 us
    all_to_all x3, waiting for transfers between devices, gather(): return lax.all_to_all(wide, axes, split_axis=0, concat_axis=0, tiled=True)  22.2 us
    dot_general x24, matrix products, dot(): lax.dot_general(a, b, (dims, ((), ())), precision=precision, preferred_el...  18.6 us
    all_to_all x1, starting transfers between devices, local(): lax.all_to_all(jnp.concatenate([sums, child], axis=1), 'pts', split_axis=...  13.7 us
    ppermute x3, starting transfers between devices, local(): sent = lax.ppermute(sent, 'x', [(j, (j + k) % nx) for j in range(nx)])  10.1 us
    all_to_all x1, starting transfers between devices, local(): lax.all_to_all(partial, 'x', split_axis=0, concat_axis=0, tiled=True)  4.55 us
    all_to_all x1, waiting for transfers between devices, local(): lax.all_to_all(jnp.concatenate([sums, child], axis=1), 'pts', split_axis=...  4.08 us
  transfers between devices with their start and end apart: 10, of which 4 were waited for; matrix products, arithmetic and copies ran while one was open for 20% of the time, Pallas kernels for 0%

profile of v1, /device:TPU:1, one launch (start us, length us, event | category | flops | bytes accessed | tf_op | source)
XLA Modules:
  0.0 133.5 jit_solution(4784650408229588019)
XLA Ops:
  0.7 0.8 bitcast_select_fusion
  1.5 0.7 add_add_fusion
  2.2 0.6 broadcast_in_dim.91
  2.8 13.8 %all-to-all-start = ((s32[8,16,128]{2,1,0:T(8,128)}), s32[8,16,128]{2,1,0:T(8,128)S(1)}, u32[]{:S(2)}, u32[]{:S(2)}) async-start(s32[8,16,128]{2,1,0:T(8,128)} %broadcast_in_dim.91), calls=%async_computation | async-start | bytes 131072 | tf_op jit(solution)/shard_map/all_to_all | solution.py:32
  16.6 1.7 %constant_dynamic-slice_fusion.25 = (bf16[1024,512]{1,0:T(8,128)(2,1)S(1)}, bf16[1024,512]{1,0:T(8,128)(2,1)S(1)}) fusion(bf16[1024,1024]{1,0:T(8,128)(2,1)} %param.6, s32[]{:T(128)S(6)} %select_n.154, s32[]{:T(128)S(6)} %select_n.158), kind=kLoop, calls=%fused_computation.166 | loop fusion | bytes 4194312 | tf_op jit(solution)/shard_map/dynamic_slice | solution.py:45
  18.3 2.0 %collective-permute-start = (bf16[1024,512]{1,0:T(8,128)(2,1)S(1)}, bf16[1024,512]{1,0:T(8,128)(2,1)S(1)}, u32[]{:S(2)}, u32[]{:S(2)}) collective-permute-start(bf16[1024,512]{1,0:T(8,128)(2,1)S(1)} %get-tuple-element.21), channel_id=1, source_target_pairs={{0,1},{1,0},{2,3},{3,2},{4,5},{5,4},{6,7},{7,6},{8,9},{9,8},{10,11... | collective-permute-start | bytes 3145736 | tf_op jit(solution)/shard_map/ppermute | solution.py:46
  20.5 0.1 convert_reduce_fusion.2
  20.6 0.9 constant_dynamic-slice_fusion.21
  21.5 0.6 convert_reduce_fusion.3
  22.1 0.5 convert_reduce_fusion
  22.7 0.2 convert_reduce_fusion.1
  22.9 0.2 select_reduce_fusion.2
  23.1 0.2 select_reduce_fusion.3
  23.4 0.2 reshape.164
  23.6 0.2 fusion.47
  23.8 0.9 fusion.41
  24.6 0.4 fusion.15
  25.1 0.4 convolution_add_fusion.2
  25.5 0.4 convolution_add_fusion.1
  26.0 0.4 fusion.17
  26.4 0.4 fusion.16
  26.9 0.4 fusion.2
  27.3 0.8 copy.32
  28.2 4.6 %all-to-all-start.1 = ((f32[4,256,128]{2,1,0:T(8,128)}), f32[4,256,128]{2,1,0:T(8,128)S(1)}, u32[]{:S(2)}, u32[]{:S(2)}) async-start(f32[4,256,128]{2,1,0:T(8,128)} %bitcast.148), calls=%async_computation.1 | async-start | bytes 1048576 | tf_op jit(solution)/shard_map/all_to_all | solution.py:78
  32.8 0.8 pad_maximum_fusion.1
  33.6 4.9 %collective-permute-start.2 = (bf16[2,2,128,512]{3,2,1,0:T(8,128)(2,1)}, bf16[2,2,128,512]{3,2,1,0:T(8,128)(2,1)}, u32[]{:S(2)}, u32[]{:S(2)}) collective-permute-start(bf16[2,2,128,512]{3,2,1,0:T(8,128)(2,1)} %pad_maximum_fusion.1), channel_id=1, source_target_pairs={{0,4},{2,6},{4,0},{6,2},{1,5},{3,7},{5,1},{7,3},{8,12},{10,14},{12... | collective-permute-start | bytes 1572872 | tf_op jit(solution)/shard_map/ppermute | solution.py:102
  38.5 0.8 pad_maximum_fusion.2
  39.4 2.8 %collective-permute-start.3 = (bf16[2,2,128,512]{3,2,1,0:T(8,128)(2,1)}, bf16[2,2,128,512]{3,2,1,0:T(8,128)(2,1)}, u32[]{:S(2)}, u32[]{:S(2)}) collective-permute-start(bf16[2,2,128,512]{3,2,1,0:T(8,128)(2,1)} %pad_maximum_fusion.2), channel_id=1, source_target_pairs={{0,6},{2,0},{4,2},{6,4},{1,7},{3,1},{5,3},{7,5},{8,14},{10,8},{12,... | collective-permute-start | bytes 1572872 | tf_op jit(solution)/shard_map/ppermute | solution.py:102
  42.2 0.8 pad_maximum_fusion
  43.0 2.5 %collective-permute-start.1 = (bf16[2,2,128,512]{3,2,1,0:T(8,128)(2,1)}, bf16[2,2,128,512]{3,2,1,0:T(8,128)(2,1)S(1)}, u32[]{:S(2)}, u32[]{:S(2)}) collective-permute-start(bf16[2,2,128,512]{3,2,1,0:T(8,128)(2,1)} %pad_maximum_fusion), channel_id=1, source_target_pairs={{0,2},{2,4},{4,6},{6,0},{1,3},{3,5},{5,7},{7,1},{8,10},{10,12},{12... | collective-permute-start | bytes 1572872 | tf_op jit(solution)/shard_map/ppermute | solution.py:102
  45.5 0.2 convolution_add_fusion.4
  45.7 0.2 convolution_add_fusion.6
  46.0 0.8 select_maximum_fusion
  46.8 13.7 %all-to-all-start.2 = ((f32[96,4,128]{2,1,0:T(4,128)}), f32[96,4,128]{2,1,0:T(4,128)S(1)}, u32[]{:S(2)}, u32[]{:S(2)}) async-start(f32[96,4,128]{2,1,0:T(4,128)} %select_maximum_fusion), calls=%async_computation.2 | async-start | bytes 393216 | tf_op jit(solution)/shard_map/all_to_all | solution.py:84
  60.6 1.1 fusion.38
  61.6 1.1 fusion.39
  62.7 1.1 fusion.44
  63.8 1.1 fusion.45
  64.9 1.1 fusion.36
  66.0 1.8 %fusion.37 = f32[128,512]{1,0:T(8,128)} fusion(bf16[2,2,128,512]{3,2,1,0:T(8,128)(2,1)} %collective-permute-done.3, s32[128]{0:T(128)S(1)} %get-tuple-element.36), kind=kOutput, calls=%fused_computation.77 | convolution fusion | flops 16793600 | bytes 393728 | tf_op jit(solution)/shard_map/dot_general | solution.py:14
  67.8 1.1 fusion.42
  68.8 1.8 %fusion.43 = f32[128,512]{1,0:T(8,128)} fusion(bf16[2,2,128,512]{3,2,1,0:T(8,128)(2,1)} %collective-permute-done.3, s32[128]{0:T(128)S(1)} %get-tuple-element.44), kind=kOutput, calls=%fused_computation.91 | convolution fusion | flops 16793600 | bytes 393728 | tf_op jit(solution)/shard_map/dot_general | solution.py:14
  70.6 4.1 %all-to-all-done.2 = f32[96,4,128]{2,1,0:T(4,128)S(1)} async-done(((f32[96,4,128]{2,1,0:T(4,128)}), f32[96,4,128]{2,1,0:T(4,128)S(1)}, u32[]{:S(2)}, u32[]{:S(2)}) %all-to-all-start.2) | async-done | bytes 196640 | tf_op jit(solution)/shard_map/all_to_all | solution.py:84
  74.7 0.1 reduce_sum.97
  74.9 0.7 broadcast_in_dim.175
  75.6 11.0 %all-to-all-start.3 = ((f32[96,3,128]{2,1,0:T(4,128)}), f32[96,3,128]{2,1,0:T(4,128)S(1)}, u32[]{:S(2)}, u32[]{:S(2)}) async-start(f32[96,3,128]{2,1,0:T(4,128)} %broadcast_in_dim.175), calls=%async_computation.3 | async-start | bytes 393216 | tf_op jit(solution)/shard_map/all_to_all | solution.py:32
  86.6 0.9 fusion.40
  87.6 0.9 fusion.46
  88.4 12.3 %all-to-all-done.3 = f32[96,3,128]{2,1,0:T(4,128)S(1)} async-done(((f32[96,3,128]{2,1,0:T(4,128)}), f32[96,3,128]{2,1,0:T(4,128)S(1)}, u32[]{:S(2)}, u32[]{:S(2)}) %all-to-all-start.3) | async-done | bytes 147488 | tf_op jit(solution)/shard_map/all_to_all | solution.py:32
  100.8 0.2 convolution_divide_fusion
  101.0 0.1 convolution_divide_fusion.1
  101.2 1.1 broadcast_in_dim.176
  102.3 11.2 %all-to-all-start.4 = ((f32[8,296,128]{2,1,0:T(8,128)}), f32[8,296,128]{2,1,0:T(8,128)S(1)}, u32[]{:S(2)}, u32[]{:S(2)}) async-start(f32[8,296,128]{2,1,0:T(8,128)} %broadcast_in_dim.176), calls=%async_computation.4 | async-start | bytes 2424832 | tf_op jit(solution)/shard_map/all_to_all | solution.py:32
  113.5 1.4 %fusion.11 = f32[1,128,512]{2,1,0:T(8,128)S(1)} fusion(f32[128,512]{1,0:T(8,128)S(1)} %fusion.36, f32[128,512]{1,0:T(8,128)} %fusion.37, f32[128,512]{1,0:T(8,128)S(1)} %fusion.38, f32[128,512]{1,0:T(8,128)S(1)} %fusion.39, f32[128,512]{1,0:T(8,128)} %fusion.40, f32[128,512]{1,0:T(8,128)S(1)} %convolution_add_fusion.4, ...), kind=kOutput, calls=%fused_computation.20 | convolution fusion | flops 17186816 | bytes 1966592 | tf_op jit(solution)/shard_map/dot_general | solution.py:14
  114.9 1.1 fusion.14
  116.0 0.1 maximum_divide_fusion
  116.2 1.9 %collective-permute-start.4 = (f32[128,512]{1,0:T(8,128)S(1)}, f32[128,512]{1,0:T(8,128)S(1)}, u32[]{:S(2)}, u32[]{:S(2)}) collective-permute-start(f32[128,512]{1,0:T(8,128)S(1)} %get-tuple-element.29), channel_id=1, source_target_pairs={{0,1},{1,0},{2,3},{3,2},{4,5},{5,4},{6,7},{7,6},{8,9},{9,8},{10,11... | collective-permute-start | bytes 786440 | tf_op jit(solution)/shard_map/ppermute | solution.py:112
  118.1 1.5 %collective-permute-done.4 = f32[128,512]{1,0:T(8,128)S(1)} collective-permute-done((f32[128,512]{1,0:T(8,128)S(1)}, f32[128,512]{1,0:T(8,128)S(1)}, u32[]{:S(2)}, u32[]{:S(2)}) %collective-permute-start.4) | collective-permute-done | bytes 262176 | tf_op jit(solution)/shard_map/ppermute | solution.py:112
  119.6 0.8 maximum_select_fusion
  120.5 9.9 %all-to-all-done.4 = f32[8,296,128]{2,1,0:T(8,128)S(1)} async-done(((f32[8,296,128]{2,1,0:T(8,128)}), f32[8,296,128]{2,1,0:T(8,128)S(1)}, u32[]{:S(2)}, u32[]{:S(2)}) %all-to-all-start.4) | async-done | bytes 1212448 | tf_op jit(solution)/shard_map/all_to_all | solution.py:32
  130.4 0.6 copy.28
  131.1 0.3 copy.26
  131.4 1.3 copy.29
  132.8 0.7 slice.105
  (52 shorter events, 0.8 us)
Async XLA Ops:
  2.8 19.3 %all-to-all-start = ((s32[8,16,128]{2,1,0:T(8,128)}), s32[8,16,128]{2,1,0:T(8,128)S(1)}, u32[]{:S(2)}, u32[]{:S(2)}) async-start(s32[8,16,128]{2,1,0:T(8,128)} %broadcast_in_dim.91), calls=%async_computation | async-start | bytes 131072 | tf_op jit(solution)/shard_map/all_to_all | solution.py:32
  16.6 3.9 %copy-start.7 = (s32[256]{0:T(256)S(1)}, s32[256]{0:T(256)}, u32[]{:S(2)}) copy-start(s32[256]{0:T(256)} %param.10) | copy-start | bytes 3076
  16.6 4.9 %copy-start.8 = (s32[32]{0:T(128)S(1)}, s32[32]{0:T(128)}, u32[]{:S(2)}) copy-start(s32[32]{0:T(128)} %param.11) | copy-start | bytes 388
  18.3 7.7 %collective-permute-start = (bf16[1024,512]{1,0:T(8,128)(2,1)S(1)}, bf16[1024,512]{1,0:T(8,128)(2,1)S(1)}, u32[]{:S(2)}, u32[]{:S(2)}) collective-permute-start(bf16[1024,512]{1,0:T(8,128)(2,1)S(1)} %get-tuple-element.21), channel_id=1, source_target_pairs={{0,1},{1,0},{2,3},{3,2},{4,5},{5,4},{6,7},{7,6},{8,9},{9,8},{10,11... | collective-permute-start | bytes 3145736 | tf_op jit(solution)/shard_map/ppermute | solution.py:46
  27.3 5.5 %copy-start.4 = (bf16[1,2,128,512]{3,2,1,0:T(8,128)(2,1)S(1)}, bf16[1,2,128,512]{3,2,1,0:T(8,128)(2,1)}, u32[]{:S(2)}) copy-start(bf16[1,2,128,512]{3,2,1,0:T(8,128)(2,1)} %get-tuple-element.24) | copy-start | bytes 786436
  28.1 10.4 %copy-start.3 = (bf16[1,2,128,512]{3,2,1,0:T(8,128)(2,1)S(1)}, bf16[1,2,128,512]{3,2,1,0:T(8,128)(2,1)}, u32[]{:S(2)}) copy-start(bf16[1,2,128,512]{3,2,1,0:T(8,128)(2,1)} %get-tuple-element.23) | copy-start | bytes 786436
  28.2 17.7 %all-to-all-start.1 = ((f32[4,256,128]{2,1,0:T(8,128)}), f32[4,256,128]{2,1,0:T(8,128)S(1)}, u32[]{:S(2)}, u32[]{:S(2)}) async-start(f32[4,256,128]{2,1,0:T(8,128)} %bitcast.148), calls=%async_computation.1 | async-start | bytes 1048576 | tf_op jit(solution)/shard_map/all_to_all | solution.py:78
  32.7 9.5 %copy-start.2 = (bf16[1,2,128,512]{3,2,1,0:T(8,128)(2,1)S(1)}, bf16[1,2,128,512]{3,2,1,0:T(8,128)(2,1)}, u32[]{:S(2)}) copy-start(bf16[1,2,128,512]{3,2,1,0:T(8,128)(2,1)} %get-tuple-element.22) | copy-start | bytes 786436
  32.7 12.8 %copy-start.5 = (f32[128,512]{1,0:T(8,128)S(1)}, f32[128,512]{1,0:T(8,128)}, u32[]{:S(2)}) copy-start(f32[128,512]{1,0:T(8,128)} %fusion.41) | copy-start | bytes 786436
  33.6 26.9 %collective-permute-start.2 = (bf16[2,2,128,512]{3,2,1,0:T(8,128)(2,1)}, bf16[2,2,128,512]{3,2,1,0:T(8,128)(2,1)}, u32[]{:S(2)}, u32[]{:S(2)}) collective-permute-start(bf16[2,2,128,512]{3,2,1,0:T(8,128)(2,1)} %pad_maximum_fusion.1), channel_id=1, source_target_pairs={{0,4},{2,6},{4,0},{6,2},{1,5},{3,7},{5,1},{7,3},{8,12},{10,14},{12... | collective-permute-start | bytes 1572872 | tf_op jit(solution)/shard_map/ppermute | solution.py:102
  39.4 25.5 %collective-permute-start.3 = (bf16[2,2,128,512]{3,2,1,0:T(8,128)(2,1)}, bf16[2,2,128,512]{3,2,1,0:T(8,128)(2,1)}, u32[]{:S(2)}, u32[]{:S(2)}) collective-permute-start(bf16[2,2,128,512]{3,2,1,0:T(8,128)(2,1)} %pad_maximum_fusion.2), channel_id=1, source_target_pairs={{0,6},{2,0},{4,2},{6,4},{1,7},{3,1},{5,3},{7,5},{8,14},{10,8},{12,... | collective-permute-start | bytes 1572872 | tf_op jit(solution)/shard_map/ppermute | solution.py:102
  43.0 43.6 %collective-permute-start.1 = (bf16[2,2,128,512]{3,2,1,0:T(8,128)(2,1)}, bf16[2,2,128,512]{3,2,1,0:T(8,128)(2,1)S(1)}, u32[]{:S(2)}, u32[]{:S(2)}) collective-permute-start(bf16[2,2,128,512]{3,2,1,0:T(8,128)(2,1)} %pad_maximum_fusion), channel_id=1, source_target_pairs={{0,2},{2,4},{4,6},{6,0},{1,3},{3,5},{5,7},{7,1},{8,10},{10,12},{12... | collective-permute-start | bytes 1572872 | tf_op jit(solution)/shard_map/ppermute | solution.py:102
  46.8 27.9 %all-to-all-start.2 = ((f32[96,4,128]{2,1,0:T(4,128)}), f32[96,4,128]{2,1,0:T(4,128)S(1)}, u32[]{:S(2)}, u32[]{:S(2)}) async-start(f32[96,4,128]{2,1,0:T(4,128)} %select_maximum_fusion), calls=%async_computation.2 | async-start | bytes 393216 | tf_op jit(solution)/shard_map/all_to_all | solution.py:84
  63.8 37.2 %copy-start.9 = (f32[8]{0:T(128)S(1)}, f32[8]{0:T(128)}, u32[]{:S(2)}) copy-start(f32[8]{0:T(128)} %convert_reduce_fusion.3) | copy-start | bytes 100
  75.6 25.2 %all-to-all-start.3 = ((f32[96,3,128]{2,1,0:T(4,128)}), f32[96,3,128]{2,1,0:T(4,128)S(1)}, u32[]{:S(2)}, u32[]{:S(2)}) async-start(f32[96,3,128]{2,1,0:T(4,128)} %broadcast_in_dim.175), calls=%async_computation.3 | async-start | bytes 393216 | tf_op jit(solution)/shard_map/all_to_all | solution.py:32
  86.6 15.7 %copy-start.6 = (bf16[2,2,128,512]{3,2,1,0:T(8,128)(2,1)}, bf16[2,2,128,512]{3,2,1,0:T(8,128)(2,1)S(1)}, u32[]{:S(2)}) copy-start(bf16[2,2,128,512]{3,2,1,0:T(8,128)(2,1)S(1)} %collective-permute-done.1) | copy-start | bytes 1572868
  102.3 28.0 %all-to-all-start.4 = ((f32[8,296,128]{2,1,0:T(8,128)}), f32[8,296,128]{2,1,0:T(8,128)S(1)}, u32[]{:S(2)}, u32[]{:S(2)}) async-start(f32[8,296,128]{2,1,0:T(8,128)} %broadcast_in_dim.176), calls=%async_computation.4 | async-start | bytes 2424832 | tf_op jit(solution)/shard_map/all_to_all | solution.py:32
  113.5 1.4 %copy-start = (f32[128,512]{1,0:T(8,128)S(1)}, f32[128,512]{1,0:T(8,128)}, u32[]{:S(2)}) copy-start(f32[128,512]{1,0:T(8,128)} %fusion.43) | copy-start | bytes 786436
  113.5 1.4 %copy-start.1 = (f32[128,512]{1,0:T(8,128)S(1)}, f32[128,512]{1,0:T(8,128)}, u32[]{:S(2)}) copy-start(f32[128,512]{1,0:T(8,128)} %fusion.46) | copy-start | bytes 786436
  116.2 3.4 %collective-permute-start.4 = (f32[128,512]{1,0:T(8,128)S(1)}, f32[128,512]{1,0:T(8,128)S(1)}, u32[]{:S(2)}, u32[]{:S(2)}) collective-permute-start(f32[128,512]{1,0:T(8,128)S(1)} %get-tuple-element.29), channel_id=1, source_target_pairs={{0,1},{1,0},{2,3},{3,2},{4,5},{5,4},{6,7},{7,6},{8,9},{9,8},{10,11... | collective-permute-start | bytes 786440 | tf_op jit(solution)/shard_map/ppermute | solution.py:112

commit v2 on v0

v2 whole, which is shorter than its diff:
```python
import jax
import jax.numpy as jnp
from jax import lax
from jax.experimental import pallas as pl
from jax.experimental.pallas import tpu as pltpu
from jax.sharding import Mesh, PartitionSpec as P

K2 = 256
K3 = 32
K4 = 8
LANES = 128
F32 = jnp.float32
BF16 = jnp.bfloat16
I32 = jnp.int32


def dot(a, b, precision=None):
    return lax.dot_general(
        a, b, (((1,), (0,)), ((), ())), precision=precision, preferred_element_type=F32
    )


def iota(shape, axis):
    return lax.broadcasted_iota(I32, shape, axis)


def whole(shape):
    return pl.BlockSpec(shape, lambda i, pos: (0,) * len(shape))


def call(body, pos, args, in_specs, out_shapes, flops=0, limit=32):
    single = not isinstance(out_shapes, (list, tuple))
    shapes = [out_shapes] if single else list(out_shapes)
    moved = sum(a.size * a.dtype.itemsize for a in args) + sum(
        s.size * s.dtype.itemsize for s in shapes
    )
    out = pl.pallas_call(
        body,
        grid_spec=pltpu.PrefetchScalarGridSpec(
            num_scalar_prefetch=1,
            grid=(1,),
            in_specs=in_specs,
            out_specs=[whole(s.shape) for s in shapes],
        ),
        out_shape=shapes,
        compiler_params=pltpu.CompilerParams(vmem_limit_bytes=limit * 2**20),
        cost_estimate=pl.CostEstimate(flops=flops, bytes_accessed=moved, transcendentals=0),
    )(pos, *args)
    return out[0] if single else out


def prep_kernel(pos, live, assign, parent, points, pack, give):
    groups, cap = assign.shape
    lane = iota((1, cap), 1)
    above = parent[...] * 256
    rows = [
        jnp.where(lane < live[0, b], assign[b : b + 1, :] + 1, 0) + above for b in range(groups)
    ]
    row = jnp.concatenate(rows, axis=0)
    for d in range(groups):
        pack[d] = row
    give[...] = points[...]


def replicated_count(hits):
    return dot(hits.astype(BF16), jnp.ones((hits.shape[1], LANES), BF16))


def hits_of(known, block, kdev):
    ks = iota((kdev, LANES), 0) + 1
    total = jnp.zeros((kdev, LANES), F32)
    for s in range(known.shape[0]):
        ids = known[s, pl.ds(block, 1), :] & 255
        total = total + jnp.where(ids == ks, 1.0, 0.0)
    return total


def main_kernel(pos, known, mine, theirs, out, child):
    groups, kdev = known.shape[0], known.shape[2]
    nx, cols = out.shape[0], out.shape[2]
    x, c = pos[0], pos[1]
    ks = iota((kdev, LANES), 0) + 1
    k2s = iota((K2, kdev), 0)
    total = jnp.zeros((K2, nx * cols), F32)
    children = jnp.zeros((K2, kdev), F32)
    for pair in range(groups // 2):
        lefts, parts = [], ([], [], [])
        for b in (2 * pair, 2 * pair + 1):
            inverse = 1.0 / replicated_count(hits_of(known, b, kdev))
            ids = [known[2 * x + core, b : b + 1, :] & 255 for core in (c, 1 - c)]
            onehot = jnp.concatenate(
                [jnp.where(v == ks, 1.0, 0.0).astype(BF16) for v in ids], axis=1
            )
            rows = slice(b * kdev, (b + 1) * kdev)
            sums = dot(onehot, jnp.concatenate([mine[rows, :], theirs[rows, :]], axis=0))
            sums = sums * jnp.concatenate([inverse] * nx, axis=1)
            hi = sums.astype(BF16)
            rest = sums - hi.astype(F32)
            mid = rest.astype(BF16)
            low = (rest - mid.astype(F32)).astype(BF16)
            for store, part in zip(parts, (hi, mid, low)):
                store.append(part)
            left = jnp.where((known[b, 0:1, :] >> 8) == k2s, 1.0, 0.0)
            children = children + left
            lefts.append(left.astype(BF16))
        left = jnp.concatenate(lefts, axis=1)
        for part in parts:
            total = total + dot(left, jnp.concatenate(part, axis=0))
    for j in range(nx):
        out[j] = total[:, j * cols : (j + 1) * cols]
    counts = replicated_count(children)
    ny = child.shape[0]
    rows = K2 // ny
    diagonal = iota((rows, LANES), 0) == iota((rows, LANES), 1)
    for j in range(ny):
        row = jnp.sum(
            jnp.where(diagonal, counts[j * rows : (j + 1) * rows], 0.0), axis=0, keepdims=True
        )
        child[j] = jnp.broadcast_to(row, (8, LANES))


def x_sum_kernel(pos, parts, child, out):
    ny = out.shape[0]
    rows = out.shape[1] - 8
    for j in range(ny):
        part = slice(j * rows, (j + 1) * rows)
        total = parts[0, part, :]
        for s in range(1, parts.shape[0]):
            total = total + parts[s, part, :]
        out[j, :rows] = total
        out[j, rows:] = child[j]


def y_sum_kernel(pos, parts, out):
    total = parts[0]
    for s in range(1, parts.shape[0]):
        total = total + parts[s]
    for s in range(out.shape[0]):
        out[s] = total


def z_sum_kernel(pos, parts, out):
    total = parts[0]
    for s in range(1, parts.shape[0]):
        total = total + parts[s]
    rows = out.shape[1]
    diagonal = iota((rows, LANES), 0) == iota((rows, LANES), 1)
    count = jnp.sum(
        jnp.where(diagonal, total[rows : rows + 1, :], 0.0), axis=1, keepdims=True
    )
    mean = total[:rows] / count
    for s in range(out.shape[0]):
        out[s] = mean


def mean_of(rows, parents, number):
    onehot = jnp.where(parents == iota((number, parents.shape[1]), 0), 1.0, 0.0)
    sums = dot(onehot, rows, lax.Precision.HIGHEST)
    return sums / jnp.sum(onehot, axis=1, keepdims=True)


def upper_kernel(pos, two, parent_three, parent_four, out):
    three = mean_of(two[...], parent_three[...], K3)
    four = mean_of(three, parent_four[...], K4)
    for s in range(out.shape[0]):
        out[s, :K2] = two[...]
        out[s, K2 : K2 + K3] = three
        out[s, K2 + K3 :] = four


def final_kernel(pos, kept, got, two, three, four):
    nx, cols = kept.shape[0], kept.shape[2]
    for part, core in ((kept, pos[1]), (got, 1 - pos[1])):
        for j in range(nx):
            at = pl.ds(pl.multiple_of((core * nx + j) * cols, cols), cols)
            two[:, at] = part[j, :K2]
            three[:, at] = part[j, K2 : K2 + K3]
            four[:, at] = part[j, K2 + K3 :]


def send_kernel(pos, a, b, c, after, to_a, to_b, to_c):
    to_a[...] = a[0]
    to_b[...] = b[0]
    to_c[...] = c[0]


def one_kernel(pos, known, own, *refs):
    arrived, (keep, give) = refs[:-2], refs[-2:]
    x, c = pos[0], pos[1]
    kdev = keep.shape[0]
    nx = len(arrived) + 1
    ks = iota((kdev, LANES), 0) + 1
    for out, core in ((keep, c), (give, 1 - c)):
        at = pl.ds(pl.multiple_of(core * kdev, kdev), kdev)
        onehots, rows = [], []
        for k in range(nx):
            source = lax.rem(x + nx - k, nx)
            ids = known[2 * source + c, pl.ds(2 * x + core, 1), :] & 255
            onehots.append(jnp.where(ids == ks, 1.0, 0.0).astype(BF16))
            rows.append(own[0, at, :] if k == 0 else arrived[k - 1][at, :])
        out[...] = dot(jnp.concatenate(onehots, axis=1), jnp.concatenate(rows, axis=0))


def one_mean_kernel(pos, known, keep, got, out):
    kdev = keep.shape[0]
    count = replicated_count(hits_of(known, 2 * pos[0] + pos[1], kdev))
    for j in range(out.shape[1] // LANES):
        at = slice(j * LANES, (j + 1) * LANES)
        out[:, at] = (keep[:, at] + got[:, at]) / count


def exchange(rows, axes):
    return lax.all_to_all(rows, axes, split_axis=0, concat_axis=0, tiled=True)


def swap(rows):
    return lax.ppermute(rows, "c", [(0, 1), (1, 0)])


def local(points, send_counts, assign_one, parent_two, parent_three, parent_four):
    nx, nc, ny, nz = (lax.axis_size(a) for a in ("x", "c", "y", "z"))
    groups = nx * nc
    slots, depth = points.shape
    cap = slots // groups
    kdev = parent_two.shape[0]
    half = depth // nc
    cols = half // nx
    rows = K2 // ny
    pos = jnp.stack([lax.axis_index("x"), lax.axis_index("c")]).astype(I32)
    shape = jax.ShapeDtypeStruct

    pack, give = call(
        prep_kernel,
        pos,
        (send_counts, assign_one.reshape(groups, cap), parent_two.reshape(1, kdev), points),
        [
            pl.BlockSpec(memory_space=pltpu.SMEM),
            whole((groups, cap)),
            whole((1, kdev)),
            pl.BlockSpec((slots, half), lambda i, pos: (0, 1 - pos[1])),
        ],
        (shape((groups, groups, cap), I32), shape((slots, half), BF16)),
    )
    known = exchange(pack, ("x", "c"))
    theirs = swap(give)

    partial, child = call(
        main_kernel,
        pos,
        (known, points, theirs),
        [
            whole((groups, groups, cap)),
            pl.BlockSpec((slots, half), lambda i, pos: (0, pos[1])),
            whole((slots, half)),
        ],
        (shape((nx, K2, cols), F32), shape((ny, 8, LANES), F32)),
        flops=2 * (2 * slots * kdev * half + 3 * K2 * slots * half),
    )
    partial = exchange(partial, "x")
    sums = call(
        x_sum_kernel,
        pos,
        (partial, child),
        [whole((nx, K2, cols)), whole((ny, 8, LANES))],
        shape((ny, rows + 8, cols), F32),
    )
    byx = points.reshape(nx, nc * cap, depth)
    sent = call(
        send_kernel,
        pos,
        (byx, byx, byx, sums),
        [
            pl.BlockSpec((1, nc * cap, depth), lambda i, pos, k=k: (lax.rem(pos[0] + k, nx), 0, 0))
            for k in range(1, nx)
        ]
        + [pl.BlockSpec(memory_space=pl.ANY)],
        [shape((nc * cap, depth), BF16)] * (nx - 1),
    )
    arrived = [
        lax.ppermute(v, "x", [(j, (j + k) % nx) for j in range(nx)])
        for k, v in zip(range(1, nx), sent)
    ]

    sums = exchange(sums, "y")
    sums = call(
        y_sum_kernel,
        pos,
        (sums,),
        [whole((ny, rows + 8, cols))],
        shape((nz, rows + 8, cols), F32),
    )
    sums = exchange(sums, "z")
    two = call(
        z_sum_kernel, pos, (sums,), [whole((nz, rows + 8, cols))], shape((ny, rows, cols), F32)
    )
    two = exchange(two, "y").reshape(K2, cols)
    height = K2 + K3 + K4
    upper = call(
        upper_kernel,
        pos,
        (two, parent_three.reshape(1, K2), parent_four.reshape(1, K3)),
        [whole((K2, cols)), whole((1, K2)), whole((1, K3))],
        shape((nx, height, cols), F32),
    )
    upper = exchange(upper, "x")
    other = swap(upper)
    two, three, four = call(
        final_kernel,
        pos,
        (upper, other),
        [whole((nx, height, cols))] * 2,
        (shape((K2, depth), F32), shape((K3, depth), F32), shape((K4, depth), F32)),
    )

    keep, give = call(
        one_kernel,
        pos,
        (known, byx, *arrived),
        [
            whole((groups, groups, cap)),
            pl.BlockSpec((1, nc * cap, depth), lambda i, pos: (pos[0], 0, 0)),
        ]
        + [whole((nc * cap, depth))] * (nx - 1),
        (shape((kdev, depth), F32), shape((kdev, depth), F32)),
        flops=2 * slots * kdev * depth,
    )
    one = call(
        one_mean_kernel,
        pos,
        (known, keep, swap(give)),
        [whole((groups, groups, cap)), whole((kdev, depth)), whole((kdev, depth))],
        shape((kdev, depth), F32),
    )
    return one, two, three, four


def solution(mesh):
    npts, groups = mesh.devices.shape
    ny = min(8, npts)
    fine = Mesh(mesh.devices.reshape(ny, npts // ny, groups // 2, 2), ("y", "z", "x", "c"))
    every = ("y", "z", "x", "c")
    placed = (P(every, None), P(every, None), P(every), P(every), P(), P())
    return jax.shard_map(
        local,
        mesh=fine,
        in_specs=placed,
        out_specs=(P(every, None), P(), P(), P()),
        check_vma=False,
    )
```

time: 543 us -> 130 us (0.24)
  waiting for transfers between devices: 378 us -> 1.88 us
  blocking collectives: 138 us -> 75.8 us
  starting transfers between devices: 4.2 us -> 32.8 us
  Pallas kernels: 0 us -> 14.1 us
  between operations: 14.1 us -> 0.8 us
    psum x1 -> x0, waiting for transfers between devices: 352 us -> none  [local(): lax.psum((partial_two, jnp.sum(onehot_two, axis=0)), ('pts', 'grp'))]
    psum x1 -> x0, blocking collectives: 112 us -> none  [local(): lax.psum((partial_two, jnp.sum(onehot_two, axis=0)), ('pts', 'grp'))]
    all_to_all x2 -> x5, blocking collectives: 25.8 us -> 75.8 us  [exchange(): return lax.all_to_all(rows, axes, split_axis=0, concat_axis=0, tiled=True)]
    ppermute x0 -> x6, starting transfers between devices: none -> 29.5 us  [the longest x3 21.1 us: swap(): return lax.ppermute(rows, 'c', [(0, 1), (1, 0)])]
    all_to_all x1, waiting for transfers between devices: 25.7 us -> 0.01 us  [exchange(): return lax.all_to_all(rows, axes, split_axis=0, concat_axis=0, tiled=True)]
    pallas_call x0 -> x10, Pallas kernels: none -> 14.1 us  [call(): pl.pallas_call(body, grid_spec=pltpu.PrefetchScalarGridSpec(num_scalar_pr...]
  transfers between devices with their start and end apart: 2 -> 7, of which waited for: 2 -> 1; matrix products, arithmetic and copies ran while one was open for 0% -> 0% of each run, Pallas kernels for 0% -> 5%
where the time goes in v2:
time: 130 us; the launch traced here: 129 us
  blocking collectives  75.8 us (58%)
  starting transfers between devices  32.8 us (25%)
  Pallas kernels  14.1 us (11%)
  local copies, waits for them, and re-layouts  3.6 us (3%)
  waiting for transfers between devices  1.88 us (1%)
    all_to_all x5, blocking collectives, exchange(): return lax.all_to_all(rows, axes, split_axis=0, concat_axis=0, tiled=True)  75.8 us
    ppermute x3, starting transfers between devices, swap(): return lax.ppermute(rows, 'c', [(0, 1), (1, 0)])  21.1 us
    pallas_call x10, Pallas kernels, call(): pl.pallas_call(body, grid_spec=pltpu.PrefetchScalarGridSpec(num_scalar_pr...  14.1 us
    ppermute x3, starting transfers between devices, local(): lax.ppermute(v, 'x', [(j, (j + k) % nx) for j in range(nx)])  8.4 us
    unnamed x14, local copies, waits for them, and re-layouts  3.6 us
    all_to_all x1, starting transfers between devices, exchange(): return lax.all_to_all(rows, axes, split_axis=0, concat_axis=0, tiled=True)  3.37 us
  transfers between devices with their start and end apart: 7, of which 1 were waited for; matrix products, arithmetic and copies ran while one was open for 0% of the time, Pallas kernels for 5%

profile of v2, /device:TPU:1, one launch (start us, length us, event | category | flops | bytes accessed | tf_op | source)
XLA Modules:
  0.0 129.1 jit_solution(16737614276516866001)
XLA Ops:
  0.6 0.1 pad_add_fusion.pos
  0.7 0.0 copy-start
  0.7 1.6 %copy-done = bf16[1024,1024]{1,0:T(8,128)(2,1)S(1)} copy-done((bf16[1024,1024]{1,0:T(8,128)(2,1)S(1)}, bf16[1024,1024]{1,0:T(8,128)(2,1)}, u32[]{:S(2)}) %copy-start) | copy-done | bytes 2097176
  2.3 0.0 copy-start.2
  2.3 0.7 copy-done.2
  3.0 0.0 copy-start.4
  3.0 0.7 copy-done.4
  3.6 0.0 copy-start.5
  3.6 0.7 copy-done.5
  4.3 0.0 copy-start.1
  4.3 1.2 shard_map.93
  5.5 12.4 %collective-permute-start = (bf16[1024,512]{1,0:T(8,128)(2,1)S(1)}, bf16[1024,512]{1,0:T(8,128)(2,1)S(1)}, u32[]{:S(2)}, u32[]{:S(2)}) collective-permute-start(bf16[1024,512]{1,0:T(8,128)(2,1)S(1)} %get-tuple-element.17), channel_id=1, source_target_pairs={{0,1},{1,0},{2,3},{3,2},{4,5},{5,4},{6,7},{7,6},{8,9},{9,8},{10,11... | collective-permute-start | bytes 3145736 | tf_op jit(solution)/shard_map/ppermute | solution.py:217
  17.9 7.1 %all_to_all.30.known = s32[8,8,128]{2,1,0:T(8,128)S(1)} all-to-all(s32[8,8,128]{2,1,0:T(8,128)S(1)} %get-tuple-element.16), channel_id=1, replica_groups=mesh['y'=8,'z'=12,'x'=4,'c'=2] {'x','c'}, dimensions={0} | all-to-all | bytes 65536 | tf_op jit(solution)/shard_map/all_to_all | solution.py:213
  25.0 0.0 collective-permute-done.theirs
  25.0 0.0 copy-done.1
  25.0 2.6 %shard_map.94 = (f32[4,256,128]{2,1,0:T(8,128)S(1)}, f32[8,8,128]{2,1,0:T(8,128)S(1)}) custom-call(s32[2]{0:T(128)S(1)} %pad_add_fusion.pos, s32[8,8,128]{2,1,0:T(8,128)S(1)} %all_to_all.30.known, bf16[1024,1024]{1,0:T(8,128)(2,1)S(1)} %copy-done.1, bf16[1024,512]{1,0:T(8,128)(2,1)S(1)} %collective-permute-done.theirs), custom_call_target="tpu_custom_call" | custom-call | flops 1073741824 | bytes 3735552 | tf_op jit(solution)/shard_map/pallas_call | solution.py:37
  27.6 10.9 %all_to_all.31.parts = f32[4,256,128]{2,1,0:T(8,128)S(1)} all-to-all(f32[4,256,128]{2,1,0:T(8,128)S(1)} %get-tuple-element.18), channel_id=1, replica_groups=mesh['y'=8,'z'=12,'x'=4,'c'=2] {'x'}, dimensions={0} | all-to-all | bytes 1048576 | tf_op jit(solution)/shard_map/all_to_all | solution.py:213
  38.5 0.6 shard_map.95.after
  39.1 10.7 %all_to_all.32.parts = f32[8,40,128]{2,1,0:T(8,128)S(1)} all-to-all(f32[8,40,128]{2,1,0:T(8,128)S(1)} %shard_map.95.after), channel_id=1, replica_groups=mesh['y'=8,'z'=12,'x'=4,'c'=2] {'y'}, dimensions={0} | all-to-all | bytes 327680 | tf_op jit(solution)/shard_map/all_to_all | solution.py:213
  49.8 0.6 shard_map.99
  50.4 23.5 %all_to_all.33.parts = f32[12,40,128]{2,1,0:T(8,128)S(1)} all-to-all(f32[12,40,128]{2,1,0:T(8,128)S(1)} %shard_map.99), channel_id=1, replica_groups=mesh['y'=8,'z'=12,'x'=4,'c'=2] {'z'}, dimensions={0} | all-to-all | bytes 491520 | tf_op jit(solution)/shard_map/all_to_all | solution.py:213
  73.9 1.3 %shard_map.100 = f32[8,32,128]{2,1,0:T(8,128)} custom-call(s32[2]{0:T(128)S(1)} %pad_add_fusion.pos, f32[12,40,128]{2,1,0:T(8,128)S(1)} %all_to_all.33.parts), custom_call_target="tpu_custom_call" | custom-call | bytes 376832 | tf_op jit(solution)/shard_map/pallas_call | solution.py:37
  75.2 3.4 %all-to-all-start.4 = ((f32[8,32,128]{2,1,0:T(8,128)}), f32[8,32,128]{2,1,0:T(8,128)S(1)}, u32[]{:S(2)}, u32[]{:S(2)}) async-start(f32[8,32,128]{2,1,0:T(8,128)} %shard_map.100), calls=%async_computation.4 | async-start | bytes 262144 | tf_op jit(solution)/shard_map/all_to_all | solution.py:213
  78.6 0.0 copy-start.3
  78.6 0.0 copy-start.6
  78.6 1.8 %shard_map.96 = (bf16[256,1024]{1,0:T(8,128)(2,1)}, bf16[256,1024]{1,0:T(8,128)(2,1)}, bf16[256,1024]{1,0:T(8,128)(2,1)}) custom-call(s32[2]{0:T(128)S(1)} %pad_add_fusion.pos, bf16[4,256,1024]{2,1,0:T(8,128)(2,1)S(1)} %bitcast.8, bf16[4,256,1024]{2,1,0:T(8,128)(2,1)S(1)} %bitcast.9, bf16[4,256,1024]{2,1,0:T(8,128)(2,1)S(1)} %bitcast.10, ...), custom_call_target="tpu_custom_call" | custom-call | bytes 8028160 | tf_op jit(solution)/shard_map/pallas_call | solution.py:37
  80.4 2.2 %collective-permute-start.1 = (bf16[256,1024]{1,0:T(8,128)(2,1)}, bf16[256,1024]{1,0:T(8,128)(2,1)S(1)}, u32[]{:S(2)}, u32[]{:S(2)}) collective-permute-start(bf16[256,1024]{1,0:T(8,128)(2,1)} %get-tuple-element.20), channel_id=1, source_target_pairs={{0,2},{2,4},{4,6},{6,0},{1,3},{3,5},{5,7},{7,1},{8,10},{10,12},{12... | collective-permute-start | bytes 1572872 | tf_op jit(solution)/shard_map/ppermute | solution.py:280
  82.6 3.7 %collective-permute-start.2 = (bf16[256,1024]{1,0:T(8,128)(2,1)}, bf16[256,1024]{1,0:T(8,128)(2,1)S(1)}, u32[]{:S(2)}, u32[]{:S(2)}) collective-permute-start(bf16[256,1024]{1,0:T(8,128)(2,1)} %get-tuple-element.21), channel_id=1, source_target_pairs={{0,4},{2,6},{4,0},{6,2},{1,5},{3,7},{5,1},{7,3},{8,12},{10,14},{12... | collective-permute-start | bytes 1572872 | tf_op jit(solution)/shard_map/ppermute | solution.py:280
  86.3 2.5 %collective-permute-start.3 = (bf16[256,1024]{1,0:T(8,128)(2,1)}, bf16[256,1024]{1,0:T(8,128)(2,1)}, u32[]{:S(2)}, u32[]{:S(2)}) collective-permute-start(bf16[256,1024]{1,0:T(8,128)(2,1)} %get-tuple-element.22), channel_id=1, source_target_pairs={{0,6},{2,0},{4,2},{6,4},{1,7},{3,1},{5,3},{7,5},{8,14},{10,8},{12,... | collective-permute-start | bytes 1572872 | tf_op jit(solution)/shard_map/ppermute | solution.py:280
  88.8 0.0 all-to-all-done.4
  88.8 0.0 copy-done.3
  88.8 0.0 copy-done.6
  88.9 0.9 shard_map.101
  89.7 23.5 %all_to_all.34.kept = f32[4,296,128]{2,1,0:T(8,128)S(1)} all-to-all(f32[4,296,128]{2,1,0:T(8,128)S(1)} %shard_map.101), channel_id=1, replica_groups=mesh['y'=8,'z'=12,'x'=4,'c'=2] {'x'}, dimensions={0} | all-to-all | bytes 1212416 | tf_op jit(solution)/shard_map/all_to_all | solution.py:213
  113.3 6.7 %collective-permute-start.5 = (f32[4,296,128]{2,1,0:T(8,128)S(1)}, f32[4,296,128]{2,1,0:T(8,128)S(1)}, u32[]{:S(2)}, u32[]{:S(2)}) collective-permute-start(f32[4,296,128]{2,1,0:T(8,128)S(1)} %all_to_all.34.kept), channel_id=1, source_target_pairs={{0,1},{1,0},{2,3},{3,2},{4,5},{5,4},{6,7},{7,6},{8,9},{9,8},{10,11... | collective-permute-start | bytes 1818632 | tf_op jit(solution)/shard_map/ppermute | solution.py:217
  120.0 0.0 collective-permute-done.1.refs_0_
  120.0 0.0 collective-permute-done.2.refs_1_
  120.0 0.0 collective-permute-done.3.refs_2_
  120.0 2.0 %shard_map.97 = (f32[128,1024]{1,0:T(8,128)S(1)}, f32[128,1024]{1,0:T(8,128)S(1)}) custom-call(s32[2]{0:T(128)S(1)} %pad_add_fusion.pos, s32[8,8,128]{2,1,0:T(8,128)S(1)} %all_to_all.30.known, bf16[4,256,1024]{2,1,0:T(8,128)(2,1)S(1)} %bitcast.11, bf16[256,1024]{1,0:T(8,128)(2,1)S(1)} %collective-permute-done.1.refs_0_, ...), custom_call_target="tpu_custom_call" | custom-call | flops 268435456 | bytes 4751360 | tf_op jit(solution)/shard_map/pallas_call | solution.py:37
  122.1 1.9 %collective-permute-start.4 = (f32[128,1024]{1,0:T(8,128)S(1)}, f32[128,1024]{1,0:T(8,128)S(1)}, u32[]{:S(2)}, u32[]{:S(2)}) collective-permute-start(f32[128,1024]{1,0:T(8,128)S(1)} %get-tuple-element.24), channel_id=1, source_target_pairs={{0,1},{1,0},{2,3},{3,2},{4,5},{5,4},{6,7},{7,6},{8,9},{9,8},{10,11... | collective-permute-start | bytes 1572872 | tf_op jit(solution)/shard_map/ppermute | solution.py:217
  124.0 1.9 %collective-permute-done.4.got = f32[128,1024]{1,0:T(8,128)S(1)} collective-permute-done((f32[128,1024]{1,0:T(8,128)S(1)}, f32[128,1024]{1,0:T(8,128)S(1)}, u32[]{:S(2)}, u32[]{:S(2)}) %collective-permute-start.4) | collective-permute-done | bytes 524320 | tf_op jit(solution)/shard_map/ppermute | solution.py:217
  125.9 1.5 %shard_map.98 = f32[128,1024]{1,0:T(8,128)} custom-call(s32[2]{0:T(128)S(1)} %pad_add_fusion.pos, s32[8,8,128]{2,1,0:T(8,128)S(1)} %all_to_all.30.known, f32[128,1024]{1,0:T(8,128)S(1)} %get-tuple-element.23.keep, f32[128,1024]{1,0:T(8,128)S(1)} %collective-permute-done.4.got), custom_call_target="tpu_custom_call" | custom-call | bytes 1605632 | tf_op jit(solution)/shard_map/pallas_call | solution.py:37
  127.4 0.0 collective-permute-done.5.got
  127.4 1.7 %shard_map.102 = (f32[256,1024]{1,0:T(8,128)}, f32[32,1024]{1,0:T(8,128)}, f32[8,1024]{1,0:T(8,128)}) custom-call(s32[2]{0:T(128)S(1)} %pad_add_fusion.pos, f32[4,296,128]{2,1,0:T(8,128)S(1)} %all_to_all.34.kept, f32[4,296,128]{2,1,0:T(8,128)S(1)} %collective-permute-done.5.got), custom_call_target="tpu_custom_call" | custom-call | bytes 2424832 | tf_op jit(solution)/shard_map/pallas_call | solution.py:37
Async XLA Ops:
  0.7 1.6 %copy-start = (bf16[1024,1024]{1,0:T(8,128)(2,1)S(1)}, bf16[1024,1024]{1,0:T(8,128)(2,1)}, u32[]{:S(2)}) copy-start(bf16[1024,1024]{1,0:T(8,128)(2,1)} %mine.1) | copy-start | bytes 6291460
  2.3 0.7 copy-start.2
  3.0 0.7 copy-start.4
  3.6 0.7 copy-start.5
  4.3 20.7 %copy-start.1 = (bf16[1024,1024]{1,0:T(8,128)(2,1)S(1)}, bf16[1024,1024]{1,0:T(8,128)(2,1)}, u32[]{:S(2)}) copy-start(bf16[1024,1024]{1,0:T(8,128)(2,1)} %mine.1) | copy-start | bytes 6291460
  5.5 19.5 %collective-permute-start = (bf16[1024,512]{1,0:T(8,128)(2,1)S(1)}, bf16[1024,512]{1,0:T(8,128)(2,1)S(1)}, u32[]{:S(2)}, u32[]{:S(2)}) collective-permute-start(bf16[1024,512]{1,0:T(8,128)(2,1)S(1)} %get-tuple-element.17), channel_id=1, source_target_pairs={{0,1},{1,0},{2,3},{3,2},{4,5},{5,4},{6,7},{7,6},{8,9},{9,8},{10,11... | collective-permute-start | bytes 3145736 | tf_op jit(solution)/shard_map/ppermute | solution.py:217
  75.2 13.6 %all-to-all-start.4 = ((f32[8,32,128]{2,1,0:T(8,128)}), f32[8,32,128]{2,1,0:T(8,128)S(1)}, u32[]{:S(2)}, u32[]{:S(2)}) async-start(f32[8,32,128]{2,1,0:T(8,128)} %shard_map.100), calls=%async_computation.4 | async-start | bytes 262144 | tf_op jit(solution)/shard_map/all_to_all | solution.py:213
  78.6 10.3 %copy-start.3 = (s32[256]{0:T(256)S(1)}, s32[256]{0:T(256)}, u32[]{:S(2)}) copy-start(s32[256]{0:T(256)} %param.10) | copy-start | bytes 3076
  78.6 10.3 %copy-start.6 = (s32[32]{0:T(128)S(1)}, s32[32]{0:T(128)}, u32[]{:S(2)}) copy-start(s32[32]{0:T(128)} %param.11) | copy-start | bytes 388
  80.4 39.6 %collective-permute-start.1 = (bf16[256,1024]{1,0:T(8,128)(2,1)}, bf16[256,1024]{1,0:T(8,128)(2,1)S(1)}, u32[]{:S(2)}, u32[]{:S(2)}) collective-permute-start(bf16[256,1024]{1,0:T(8,128)(2,1)} %get-tuple-element.20), channel_id=1, source_target_pairs={{0,2},{2,4},{4,6},{6,0},{1,3},{3,5},{5,7},{7,1},{8,10},{10,12},{12... | collective-permute-start | bytes 1572872 | tf_op jit(solution)/shard_map/ppermute | solution.py:280
  82.6 37.4 %collective-permute-start.2 = (bf16[256,1024]{1,0:T(8,128)(2,1)}, bf16[256,1024]{1,0:T(8,128)(2,1)S(1)}, u32[]{:S(2)}, u32[]{:S(2)}) collective-permute-start(bf16[256,1024]{1,0:T(8,128)(2,1)} %get-tuple-element.21), channel_id=1, source_target_pairs={{0,4},{2,6},{4,0},{6,2},{1,5},{3,7},{5,1},{7,3},{8,12},{10,14},{12... | collective-permute-start | bytes 1572872 | tf_op jit(solution)/shard_map/ppermute | solution.py:280
  86.3 33.7 %collective-permute-start.3 = (bf16[256,1024]{1,0:T(8,128)(2,1)}, bf16[256,1024]{1,0:T(8,128)(2,1)}, u32[]{:S(2)}, u32[]{:S(2)}) collective-permute-start(bf16[256,1024]{1,0:T(8,128)(2,1)} %get-tuple-element.22), channel_id=1, source_target_pairs={{0,6},{2,0},{4,2},{6,4},{1,7},{3,1},{5,3},{7,5},{8,14},{10,8},{12,... | collective-permute-start | bytes 1572872 | tf_op jit(solution)/shard_map/ppermute | solution.py:280
  113.3 14.1 %collective-permute-start.5 = (f32[4,296,128]{2,1,0:T(8,128)S(1)}, f32[4,296,128]{2,1,0:T(8,128)S(1)}, u32[]{:S(2)}, u32[]{:S(2)}) collective-permute-start(f32[4,296,128]{2,1,0:T(8,128)S(1)} %all_to_all.34.kept), channel_id=1, source_target_pairs={{0,1},{1,0},{2,3},{3,2},{4,5},{5,4},{6,7},{7,6},{8,9},{9,8},{10,11... | collective-permute-start | bytes 1818632 | tf_op jit(solution)/shard_map/ppermute | solution.py:217
  122.1 3.8 %collective-permute-start.4 = (f32[128,1024]{1,0:T(8,128)S(1)}, f32[128,1024]{1,0:T(8,128)S(1)}, u32[]{:S(2)}, u32[]{:S(2)}) collective-permute-start(f32[128,1024]{1,0:T(8,128)S(1)} %get-tuple-element.24), channel_id=1, source_target_pairs={{0,1},{1,0},{2,3},{3,2},{4,5},{5,4},{6,7},{7,6},{8,9},{9,8},{10,11... | collective-permute-start | bytes 1572872 | tf_op jit(solution)/shard_map/ppermute | solution.py:217

commit v3 on v2

v3 whole, which is shorter than its diff:
```python
import functools

import jax
import jax.numpy as jnp
from jax import lax
from jax.experimental import pallas as pl
from jax.experimental.pallas import tpu as pltpu
from jax.sharding import Mesh, PartitionSpec as P

K2 = 256
K3 = 32
K4 = 8
LANES = 128
F32 = jnp.float32
BF16 = jnp.bfloat16
I32 = jnp.int32


def dot(a, b, precision=None):
    return lax.dot_general(
        a, b, (((1,), (0,)), ((), ())), precision=precision, preferred_element_type=F32
    )


def iota(shape, axis):
    return lax.broadcasted_iota(I32, shape, axis)


def whole(shape):
    return pl.BlockSpec(shape, lambda i, pos: (0,) * len(shape))


def call(body, pos, args, in_specs, out_shapes, flops=0, limit=24, scratch=(), far=0):
    single = not isinstance(out_shapes, (list, tuple))
    shapes = [out_shapes] if single else list(out_shapes)
    moved = sum(a.size * a.dtype.itemsize for a in args) + sum(
        s.size * s.dtype.itemsize for s in shapes
    )
    out = pl.pallas_call(
        body,
        grid_spec=pltpu.PrefetchScalarGridSpec(
            num_scalar_prefetch=1,
            grid=(1,),
            in_specs=in_specs,
            out_specs=[whole(s.shape) for s in shapes[: len(shapes) - far]]
            + [pl.BlockSpec(memory_space=pltpu.HBM)] * far,
            scratch_shapes=scratch,
        ),
        out_shape=shapes,
        compiler_params=pltpu.CompilerParams(vmem_limit_bytes=limit * 2**20),
        cost_estimate=pl.CostEstimate(flops=flops, bytes_accessed=moved, transcendentals=0),
    )(pos, *args)
    return out[0] if single else out


def prep_kernel(live, assign, parent, pack, live_s, assign_v, parent_v, sems):
    groups, cap = assign.shape
    copies = [
        pltpu.make_async_copy(source, target, sems.at[i])
        for i, (source, target) in enumerate(
            [(live, live_s), (assign, assign_v), (parent, parent_v)]
        )
    ]
    for copy in copies:
        copy.start()
    for copy in copies:
        copy.wait()
    lane = iota((1, cap), 1)
    above = parent_v[...] * 256
    rows = [
        jnp.where(lane < live_s[0, b], assign_v[b : b + 1, :] + 1, 0) + above
        for b in range(groups)
    ]
    row = jnp.concatenate(rows, axis=0)
    for d in range(groups):
        pack[d] = row


def replicated_count(hits):
    return dot(hits.astype(BF16), jnp.ones((hits.shape[1], LANES), BF16))


def hits_of(known, block, kdev):
    ks = iota((kdev, LANES), 0) + 1
    total = jnp.zeros((kdev, LANES), F32)
    for s in range(known.shape[0]):
        ids = known[s, pl.ds(block, 1), :] & 255
        total = total + jnp.where(ids == ks, 1.0, 0.0)
    return total


def main_kernel(pos, known, mine, theirs, out, child, *refs):
    sent, (weights, sems) = refs[:-2], refs[-2:]
    groups, kdev = known.shape[0], known.shape[2]
    nx, height, lanes = out.shape
    half = weights.shape[1] // 3
    x, c = pos[0], pos[1]
    copies = []
    for k, target in enumerate(sent):
        block = 2 * lax.rem(x + k, nx) + c
        at = pl.ds(pl.multiple_of(block * kdev, kdev), kdev)
        for which, rows in enumerate((mine, theirs)):
            copies.append(
                pltpu.make_async_copy(rows.at[at, :], target.at[which], sems.at[k, which])
            )
    for copy in copies:
        copy.start()
    ks = iota((kdev, LANES), 0) + 1
    k2s = iota((half, kdev), 0) + c * half
    diagonal = iota((kdev, LANES), 0) == iota((kdev, LANES), 1)
    children = jnp.zeros((half, kdev), F32)
    for b in range(groups):
        inverse = 1.0 / replicated_count(hits_of(known, b, kdev))
        inverse = jnp.sum(jnp.where(diagonal, inverse, 0.0), axis=0, keepdims=True)
        chosen = (known[b, 0:1, :] >> 8) == k2s
        children = children + jnp.where(chosen, 1.0, 0.0)
        weight = jnp.where(chosen, inverse, 0.0)
        hi = weight.astype(BF16)
        rest = weight - hi.astype(F32)
        mid = rest.astype(BF16)
        low = (rest - mid.astype(F32)).astype(BF16)
        parts = jnp.concatenate([hi, mid, low], axis=0)
        for which, core in ((0, c), (1, 1 - c)):
            ids = known[2 * x + core, b : b + 1, :] & 255
            onehot = jnp.where(ids == ks, 1.0, 0.0).astype(BF16)
            weights[which, :, b * kdev : (b + 1) * kdev] = dot(parts, onehot).astype(BF16)
    for j in range(nx):
        at = slice(j * 2 * lanes, (j + 1) * 2 * lanes)
        total = dot(weights[0], mine[:, at]) + dot(weights[1], theirs[:, at])
        total = total[:half] + total[half : 2 * half] + total[2 * half :]
        out[j, :half] = total[:, :lanes]
        out[j, half:] = total[:, lanes:]
    counts = replicated_count(children)
    ny = child.shape[0]
    rows = half // ny
    diagonal = iota((rows, LANES), 0) == iota((rows, LANES), 1)
    for j in range(ny):
        row = jnp.sum(
            jnp.where(diagonal, counts[j * rows : (j + 1) * rows], 0.0), axis=0, keepdims=True
        )
        child[j] = jnp.broadcast_to(row, (8, LANES))
    for copy in copies:
        copy.wait()


def x_sum_kernel(pos, parts, child, out):
    ny = out.shape[0]
    rows = (out.shape[1] - 8) // 2
    half = parts.shape[1] // 2
    for j in range(ny):
        for h in range(2):
            part = slice(h * half + j * rows, h * half + (j + 1) * rows)
            total = parts[0, part, :]
            for s in range(1, parts.shape[0]):
                total = total + parts[s, part, :]
            out[j, h * rows : (h + 1) * rows] = total
        out[j, 2 * rows :] = child[j]


def y_sum_kernel(pos, parts, out):
    total = parts[0]
    for s in range(1, parts.shape[0]):
        total = total + parts[s]
    for s in range(out.shape[0]):
        out[s] = total


def z_sum_kernel(pos, parts, out):
    total = parts[0]
    for s in range(1, parts.shape[0]):
        total = total + parts[s]
    rows = out.shape[1] // 2
    diagonal = iota((rows, LANES), 0) == iota((rows, LANES), 1)
    count = jnp.sum(
        jnp.where(diagonal, total[2 * rows : 2 * rows + 1, :], 0.0), axis=1, keepdims=True
    )
    for h in range(2):
        mean = total[h * rows : (h + 1) * rows] / count
        for s in range(out.shape[0]):
            out[s, h * rows : (h + 1) * rows] = mean


def mean_of(rows, parents, number):
    onehot = jnp.where(parents == iota((number, parents.shape[1]), 0), 1.0, 0.0)
    sums = dot(onehot, rows, lax.Precision.HIGHEST)
    return sums / jnp.sum(onehot, axis=1, keepdims=True)


def wide_kernel(pos, two, *refs):
    out = refs[-1]
    ny = two.shape[0]
    rows = two.shape[1] // 2
    half = out.shape[1] // 2
    for h in range(2):
        for j in range(ny):
            part = two[j, h * rows : (h + 1) * rows]
            for s in range(out.shape[0]):
                out[s, h * half + j * rows : h * half + (j + 1) * rows] = part


def final_kernel(pos, kept, got, parent_three, parent_four, two, three, four):
    nx, lanes = kept.shape[0], kept.shape[2]
    half = kept.shape[1] // 2
    for part, core in ((kept, pos[1]), (got, 1 - pos[1])):
        to = pl.ds(pl.multiple_of(core * half, half), half)
        for j in range(nx):
            for h in range(2):
                at = slice((2 * j + h) * lanes, (2 * j + h + 1) * lanes)
                two[to, at] = part[j, h * half : (h + 1) * half]
    mean = mean_of(two[...], parent_three[...], K3)
    three[...] = mean
    four[...] = mean_of(mean, parent_four[...], K4)


def one_kernel(pos, known, *refs):
    arrived, out = refs[:-1], refs[-1]
    x, c = pos[0], pos[1]
    kdev = out.shape[0]
    nx = len(arrived)
    ks = iota((kdev, LANES), 0) + 1
    onehots, rows = [], []
    for k in range(nx):
        source = lax.rem(x + nx - k, nx)
        for which, core in ((0, c), (1, 1 - c)):
            ids = known[2 * source + core, pl.ds(2 * x + c, 1), :] & 255
            onehots.append(jnp.where(ids == ks, 1.0, 0.0).astype(BF16))
            rows.append(arrived[k][which])
    sums = dot(jnp.concatenate(onehots, axis=1), jnp.concatenate(rows, axis=0))
    count = replicated_count(hits_of(known, 2 * x + c, kdev))
    for j in range(out.shape[1] // LANES):
        at = slice(j * LANES, (j + 1) * LANES)
        out[:, at] = sums[:, at] / count


def exchange(rows, axes):
    return lax.all_to_all(rows, axes, split_axis=0, concat_axis=0, tiled=True)


def swap(rows):
    return lax.ppermute(rows, "c", [(0, 1), (1, 0)])


def local(points, send_counts, assign_one, parent_two, parent_three, parent_four):
    nx, nc, ny, nz = (lax.axis_size(a) for a in ("x", "c", "y", "z"))
    groups = nx * nc
    slots, depth = points.shape
    cap = slots // groups
    kdev = parent_two.shape[0]
    half = K2 // nc
    rows = half // ny
    assert depth == 2 * nx * LANES and nc == 2 and cap == kdev == LANES
    pos = jnp.stack([lax.axis_index("x"), lax.axis_index("c")]).astype(I32)
    shape = jax.ShapeDtypeStruct

    pack = pl.pallas_call(
        prep_kernel,
        in_specs=[pl.BlockSpec(memory_space=pltpu.HBM)] * 3,
        out_specs=pl.BlockSpec(memory_space=pltpu.VMEM),
        out_shape=shape((groups, groups, cap), I32),
        scratch_shapes=[
            pltpu.SMEM((1, groups), I32),
            pltpu.VMEM((groups, cap), I32),
            pltpu.VMEM((1, kdev), I32),
            pltpu.SemaphoreType.DMA((3,)),
        ],
        compiler_params=pltpu.CompilerParams(vmem_limit_bytes=63 * 2**20),
    )(send_counts, assign_one.reshape(groups, cap), parent_two.reshape(1, kdev))
    known = exchange(pack, ("x", "c"))
    theirs = swap(points)

    partial, child, *sent = call(
        main_kernel,
        pos,
        (known, points, theirs),
        [whole((groups, groups, cap)), whole((slots, depth)), whole((slots, depth))],
        [shape((nx, 2 * half, LANES), F32), shape((ny, 8, LANES), F32)]
        + [shape((nc, cap, depth), BF16)] * nx,
        flops=2 * 6 * slots * half * depth,
        scratch=[
            pltpu.VMEM((nc, 3 * half, slots), BF16),
            pltpu.SemaphoreType.DMA((nx, nc)),
        ],
        far=nx,
    )
    partial = exchange(partial, "x")

    sums = call(
        x_sum_kernel,
        pos,
        (partial, child),
        [whole((nx, 2 * half, LANES)), whole((ny, 8, LANES))],
        shape((ny, 2 * rows + 8, LANES), F32),
    )
    arrived = [
        lax.ppermute(v, "x", [(j, (j + k) % nx) for j in range(nx)])
        for k, v in enumerate(sent)
        if k > 0
    ]

    sums = exchange(sums, "y")
    sums = call(
        y_sum_kernel,
        pos,
        (sums,),
        [whole((ny, 2 * rows + 8, LANES))],
        shape((nz, 2 * rows + 8, LANES), F32),
    )
    sums = exchange(sums, "z")
    two = call(
        z_sum_kernel, pos, (sums,), [whole((nz, 2 * rows + 8, LANES))], shape((ny, 2 * rows, LANES), F32)
    )
    two = exchange(two, "y")
    two = call(
        wide_kernel,
        pos,
        (two, *arrived),
        [whole((ny, 2 * rows, LANES))] + [pl.BlockSpec(memory_space=pl.ANY)] * len(arrived),
        shape((nx, 2 * half, LANES), F32),
    )
    two = exchange(two, "x")
    two, three, four = call(
        final_kernel,
        pos,
        (two, swap(two), parent_three.reshape(1, K2), parent_four.reshape(1, K3)),
        [whole((nx, 2 * half, LANES))] * 2 + [whole((1, K2)), whole((1, K3))],
        [shape((n, depth), F32) for n in (K2, K3, K4)],
    )
    one = call(
        one_kernel,
        pos,
        (known, sent[0], *arrived),
        [whole((groups, groups, cap))] + [whole((nc, cap, depth))] * nx,
        shape((kdev, depth), F32),
        flops=2 * slots * kdev * depth,
    )
    return one, two, three, four


def solution(mesh):
    npts, groups = mesh.devices.shape
    ny = min(8, npts)
    fine = Mesh(mesh.devices.reshape(ny, npts // ny, groups // 2, 2), ("y", "z", "x", "c"))
    every = ("y", "z", "x", "c")
    placed = (P(every, None), P(every, None), P(every), P(every), P(), P())
    return jax.shard_map(
        local,
        mesh=fine,
        in_specs=placed,
        out_specs=(P(every, None), P(), P(), P()),
        check_vma=False,
    )
```

time: 130 us -> 116 us (0.89)
  blocking collectives: 75.8 us -> 34.6 us
  waiting for transfers between devices: 1.88 us -> 21.1 us
  starting transfers between devices: 32.8 us -> 42.7 us
  local copies, waits for them, and re-layouts: 3.6 us -> 1.6 us
    all_to_all x5 -> x3, blocking collectives: 75.8 us -> 34.6 us  [exchange(): return lax.all_to_all(rows, axes, split_axis=0, concat_axis=0, tiled=True)]
    all_to_all x1 -> x3, starting transfers between devices: 3.37 us -> 18 us  [exchange(): return lax.all_to_all(rows, axes, split_axis=0, concat_axis=0, tiled=True)]
    ppermute x3, waiting for transfers between devices: 0.01 us -> 13.2 us  [local(): lax.ppermute(v, 'x', [(j, (j + k) % nx) for j in range(nx)])]
    all_to_all x1 -> x3, waiting for transfers between devices: 0.01 us -> 7.88 us  [exchange(): return lax.all_to_all(rows, axes, split_axis=0, concat_axis=0, tiled=True)]
    ppermute x3 -> x2, starting transfers between devices: 21.1 us -> 16.3 us  [swap(): return lax.ppermute(rows, 'c', [(0, 1), (1, 0)])]
    unnamed x14 -> x6, local copies, waits for them, and re-layouts: 3.6 us -> 1.6 us
    ppermute x3 -> x2, waiting for transfers between devices: 1.87 us -> 0.01 us  [swap(): return lax.ppermute(rows, 'c', [(0, 1), (1, 0)])]
    pallas_call x0 -> x1, Pallas kernels: none -> 1.34 us  [local(): pl.pallas_call(prep_kernel, in_specs=[pl.BlockSpec(memory_space=pltpu.HBM...]
  transfers between devices with their start and end apart: 7 -> 8, of which waited for: 1 -> 4; matrix products, arithmetic and copies ran while one was open for 0% -> 0% of each run, Pallas kernels for 5% -> 4%
where the time goes in v3:
time: 116 us
  starting transfers between devices  42.7 us (37%)
  blocking collectives  34.6 us (30%)
  waiting for transfers between devices  21.1 us (18%)
  Pallas kernels  14.9 us (13%)
  local copies, waits for them, and re-layouts  1.6 us (1%)
    all_to_all x3, blocking collectives, exchange(): return lax.all_to_all(rows, axes, split_axis=0, concat_axis=0, tiled=True)  34.6 us
    all_to_all x3, starting transfers between devices, exchange(): return lax.all_to_all(rows, axes, split_axis=0, concat_axis=0, tiled=True)  18 us
    ppermute x2, starting transfers between devices, swap(): return lax.ppermute(rows, 'c', [(0, 1), (1, 0)])  16.3 us
    pallas_call x7, Pallas kernels, call(): pl.pallas_call(body, grid_spec=pltpu.PrefetchScalarGridSpec(num_scalar_pr...  13.5 us
    ppermute x3, waiting for transfers between devices, local(): lax.ppermute(v, 'x', [(j, (j + k) % nx) for j in range(nx)])  13.2 us
    ppermute x3, starting transfers between devices, local(): lax.ppermute(v, 'x', [(j, (j + k) % nx) for j in range(nx)])  8.44 us
    all_to_all x3, waiting for transfers between devices, exchange(): return lax.all_to_all(rows, axes, split_axis=0, concat_axis=0, tiled=True)  7.88 us
  transfers between devices with their start and end apart: 8, of which 4 were waited for; matrix products, arithmetic and copies ran while one was open for 0% of the time, Pallas kernels for 4%

profile of v3, /device:TPU:1, one launch (start us, length us, event | category | flops | bytes accessed | tf_op | source)
XLA Modules:
  0.0 115.7 jit_solution(8228196763825954471)
XLA Ops:
  0.6 12.4 %collective-permute-start = (bf16[1024,1024]{1,0:T(8,128)(2,1)}, bf16[1024,1024]{1,0:T(8,128)(2,1)}, u32[]{:S(2)}, u32[]{:S(2)}) collective-permute-start(bf16[1024,1024]{1,0:T(8,128)(2,1)} %mine.1), channel_id=1, source_target_pairs={{0,1},{1,0},{2,3},{3,2},{4,5},{5,4},{6,7},{7,6},{8,9},{9,8},{10,11... | collective-permute-start | bytes 6291464 | tf_op jit(solution)/shard_map/ppermute | solution.py:240
  13.1 1.3 %shard_map.93 = s32[8,8,128]{2,1,0:T(8,128)} custom-call(s32[1,8]{1,0:T(1,128)} %live.1, s32[8,128]{1,0:T(8,128)} %bitcast.8, s32[1,128]{1,0:T(1,128)} %bitcast.9), custom_call_target="tpu_custom_call" | custom-call | tf_op jit(solution)/shard_map/pallas_call | solution.py:255
  14.4 3.3 %all-to-all-start = ((s32[8,8,128]{2,1,0:T(8,128)}), s32[8,8,128]{2,1,0:T(8,128)S(1)}, u32[]{:S(2)}, u32[]{:S(2)}) async-start(s32[8,8,128]{2,1,0:T(8,128)} %shard_map.93), calls=%async_computation | async-start | bytes 65536 | tf_op jit(solution)/shard_map/all_to_all | solution.py:236
  17.7 0.1 pad_add_fusion.pos
  17.8 4.6 %all-to-all-done.known = s32[8,8,128]{2,1,0:T(8,128)S(1)} async-done(((s32[8,8,128]{2,1,0:T(8,128)}), s32[8,8,128]{2,1,0:T(8,128)S(1)}, u32[]{:S(2)}, u32[]{:S(2)}) %all-to-all-start) | async-done | bytes 32800 | tf_op jit(solution)/shard_map/all_to_all | solution.py:236
  22.4 0.0 collective-permute-done.theirs
  22.4 0.0 copy-start.2
  22.4 1.6 %copy-done.2 = bf16[1024,1024]{1,0:T(8,128)(2,1)S(1)} copy-done((bf16[1024,1024]{1,0:T(8,128)(2,1)S(1)}, bf16[1024,1024]{1,0:T(8,128)(2,1)}, u32[]{:S(2)}) %copy-start.2) | copy-done | bytes 2097176
  24.0 5.9 %shard_map.94 = (f32[4,256,128]{2,1,0:T(8,128)S(1)}, f32[8,8,128]{2,1,0:T(8,128)S(1)}, bf16[2,128,1024]{2,1,0:T(8,128)(2,1)S(1)}, bf16[2,128,1024]{2,1,0:T(8,128...) custom-call(s32[2]{0:T(128)S(1)} %pad_add_fusion.pos, s32[8,8,128]{2,1,0:T(8,128)S(1)} %all-to-all-done.known, ...), custom_call_target="tpu_custom_call" | custom-call | flops 1610612736 | bytes 6881280 | tf_op jit(solution)/shard_map/pallas_call | solution.py:39
  29.9 10.9 %all_to_all.30.parts = f32[4,256,128]{2,1,0:T(8,128)S(1)} all-to-all(f32[4,256,128]{2,1,0:T(8,128)S(1)} %get-tuple-element.17), channel_id=1, replica_groups=mesh['y'=8,'z'=12,'x'=4,'c'=2] {'x'}, dimensions={0} | all-to-all | bytes 1048576 | tf_op jit(solution)/shard_map/all_to_all | solution.py:236
  40.9 0.6 shard_map.96
  41.4 10.7 %all_to_all.31.parts = f32[8,40,128]{2,1,0:T(8,128)S(1)} all-to-all(f32[8,40,128]{2,1,0:T(8,128)S(1)} %shard_map.96), channel_id=1, replica_groups=mesh['y'=8,'z'=12,'x'=4,'c'=2] {'y'}, dimensions={0} | all-to-all | bytes 327680 | tf_op jit(solution)/shard_map/all_to_all | solution.py:236
  52.1 1.3 %shard_map.97 = f32[12,40,128]{2,1,0:T(8,128)} custom-call(s32[2]{0:T(128)S(1)} %pad_add_fusion.pos, f32[8,40,128]{2,1,0:T(8,128)S(1)} %all_to_all.31.parts), custom_call_target="tpu_custom_call" | custom-call | bytes 409600 | tf_op jit(solution)/shard_map/pallas_call | solution.py:39
  53.4 11.3 %all-to-all-start.3 = ((f32[12,40,128]{2,1,0:T(8,128)}), f32[12,40,128]{2,1,0:T(8,128)S(1)}, u32[]{:S(2)}, u32[]{:S(2)}) async-start(f32[12,40,128]{2,1,0:T(8,128)} %shard_map.97), calls=%async_computation.3 | async-start | bytes 491520 | tf_op jit(solution)/shard_map/all_to_all | solution.py:236
  64.7 2.2 %collective-permute-start.1 = (bf16[2,128,1024]{2,1,0:T(8,128)(2,1)}, bf16[2,128,1024]{2,1,0:T(8,128)(2,1)S(1)}, u32[]{:S(2)}, u32[]{:S(2)}) collective-permute-start(bf16[2,128,1024]{2,1,0:T(8,128)(2,1)} %get-tuple-element.14), channel_id=1, source_target_pairs={{0,2},{2,4},{4,6},{6,0},{1,3},{3,5},{5,7},{7,1},{8,10},{10,12},{12... | collective-permute-start | bytes 1572872 | tf_op jit(solution)/shard_map/ppermute | solution.py:295
  66.9 3.7 %collective-permute-start.2 = (bf16[2,128,1024]{2,1,0:T(8,128)(2,1)S(1)}, bf16[2,128,1024]{2,1,0:T(8,128)(2,1)S(1)}, u32[]{:S(2)}, u32[]{:S(2)}) collective-permute-start(bf16[2,128,1024]{2,1,0:T(8,128)(2,1)S(1)} %get-tuple-element.15), channel_id=1, source_target_pairs={{0,4},{2,6},{4,0},{6,2},{1,5},{3,7},{5,1},{7,3},{8,12},{10,14},{12... | collective-permute-start | bytes 1572872 | tf_op jit(solution)/shard_map/ppermute | solution.py:295
  70.6 2.6 %collective-permute-start.3 = (bf16[2,128,1024]{2,1,0:T(8,128)(2,1)S(1)}, bf16[2,128,1024]{2,1,0:T(8,128)(2,1)S(1)}, u32[]{:S(2)}, u32[]{:S(2)}) collective-permute-start(bf16[2,128,1024]{2,1,0:T(8,128)(2,1)S(1)} %get-tuple-element.16), channel_id=1, source_target_pairs={{0,6},{2,0},{4,2},{6,4},{1,7},{3,1},{5,3},{7,5},{8,14},{10,8},{12,... | collective-permute-start | bytes 1572872 | tf_op jit(solution)/shard_map/ppermute | solution.py:295
  73.2 3.3 %all-to-all-done.3.parts = f32[12,40,128]{2,1,0:T(8,128)S(1)} async-done(((f32[12,40,128]{2,1,0:T(8,128)}), f32[12,40,128]{2,1,0:T(8,128)S(1)}, u32[]{:S(2)}, u32[]{:S(2)}) %all-to-all-start.3) | async-done | bytes 245792 | tf_op jit(solution)/shard_map/all_to_all | solution.py:236
  76.4 1.3 %shard_map.98 = f32[8,32,128]{2,1,0:T(8,128)} custom-call(s32[2]{0:T(128)S(1)} %pad_add_fusion.pos, f32[12,40,128]{2,1,0:T(8,128)S(1)} %all-to-all-done.3.parts), custom_call_target="tpu_custom_call" | custom-call | bytes 376832 | tf_op jit(solution)/shard_map/pallas_call | solution.py:39
  77.7 3.4 %all-to-all-start.4 = ((f32[8,32,128]{2,1,0:T(8,128)}), f32[8,32,128]{2,1,0:T(8,128)S(1)}, u32[]{:S(2)}, u32[]{:S(2)}) async-start(f32[8,32,128]{2,1,0:T(8,128)} %shard_map.98), calls=%async_computation.4 | async-start | bytes 262144 | tf_op jit(solution)/shard_map/all_to_all | solution.py:236
  81.1 0.0 collective-permute-done.1.refs_1_.refs_0_
  81.1 7.5 %collective-permute-done.2.refs_2_.refs_1_ = bf16[2,128,1024]{2,1,0:T(8,128)(2,1)S(1)} collective-permute-done((bf16[2,128,1024]{2,1,0:T(8,128)(2,1)S(1)}, bf16[2,128,1024]{2,1,0:T(8,128)(2,1)S(1)}, u32[]{:S(2)}, u32[]{:S(2)}) %collective-permute-start.2) | collective-permute-done | bytes 524320 | tf_op jit(solution)/shard_map/ppermute | solution.py:295
  88.6 5.8 %collective-permute-done.3.refs_3_.refs_2_ = bf16[2,128,1024]{2,1,0:T(8,128)(2,1)S(1)} collective-permute-done((bf16[2,128,1024]{2,1,0:T(8,128)(2,1)S(1)}, bf16[2,128,1024]{2,1,0:T(8,128)(2,1)S(1)}, u32[]{:S(2)}, u32[]{:S(2)}) %collective-permute-start.3) | collective-permute-done | bytes 524320 | tf_op jit(solution)/shard_map/ppermute | solution.py:295
  94.4 0.0 all-to-all-done.4.two
  94.4 0.6 shard_map.99
  94.9 0.0 copy-start
  95.0 0.0 copy-start.1
  95.0 13.0 %all_to_all.32.kept = f32[4,256,128]{2,1,0:T(8,128)S(1)} all-to-all(f32[4,256,128]{2,1,0:T(8,128)S(1)} %shard_map.99), channel_id=1, replica_groups=mesh['y'=8,'z'=12,'x'=4,'c'=2] {'x'}, dimensions={0} | all-to-all | bytes 1048576 | tf_op jit(solution)/shard_map/all_to_all | solution.py:236
  107.9 3.8 %collective-permute-start.4 = (f32[4,256,128]{2,1,0:T(8,128)S(1)}, f32[4,256,128]{2,1,0:T(8,128)S(1)}, u32[]{:S(2)}, u32[]{:S(2)}) collective-permute-start(f32[4,256,128]{2,1,0:T(8,128)S(1)} %all_to_all.32.kept), channel_id=1, source_target_pairs={{0,1},{1,0},{2,3},{3,2},{4,5},{5,4},{6,7},{7,6},{8,9},{9,8},{10,11... | collective-permute-start | bytes 1572872 | tf_op jit(solution)/shard_map/ppermute | solution.py:240
  111.8 1.8 %shard_map.95 = f32[128,1024]{1,0:T(8,128)} custom-call(s32[2]{0:T(128)S(1)} %pad_add_fusion.pos, s32[8,8,128]{2,1,0:T(8,128)S(1)} %all-to-all-done.known, bf16[2,128,1024]{2,1,0:T(8,128)(2,1)S(1)} %get-tuple-element.13.refs_0_, bf16[2,128,1024]{2,1,0:T(8,128)(2,1)S(1)} %collective-permute-done.1.refs_1_.refs_0_, ...), custom_call_target="tpu_custom_call" | custom-call | flops 268435456 | bytes 2654208 | tf_op jit(solution)/shard_map/pallas_call | solution.py:39
  113.6 0.0 collective-permute-done.4.got
  113.6 0.0 copy-done
  113.6 0.0 copy-done.1
  113.6 2.1 %shard_map.100 = (f32[256,1024]{1,0:T(8,128)}, f32[32,1024]{1,0:T(8,128)}, f32[8,1024]{1,0:T(8,128)}) custom-call(s32[2]{0:T(128)S(1)} %pad_add_fusion.pos, f32[4,256,128]{2,1,0:T(8,128)S(1)} %all_to_all.32.kept, f32[4,256,128]{2,1,0:T(8,128)S(1)} %collective-permute-done.4.got, s32[1,256]{1,0:T(1,128)S(1)} %bitcast.6, s32[1,32]{1,0:T(1,128)S(1)} %bitcast.7), custom_call_target="tpu_custom_call" | custom-call | bytes 2262144 | tf_op jit(solution)/shard_map/pallas_call | solution.py:39
Async XLA Ops:
  0.6 21.8 %collective-permute-start = (bf16[1024,1024]{1,0:T(8,128)(2,1)}, bf16[1024,1024]{1,0:T(8,128)(2,1)}, u32[]{:S(2)}, u32[]{:S(2)}) collective-permute-start(bf16[1024,1024]{1,0:T(8,128)(2,1)} %mine.1), channel_id=1, source_target_pairs={{0,1},{1,0},{2,3},{3,2},{4,5},{5,4},{6,7},{7,6},{8,9},{9,8},{10,11... | collective-permute-start | bytes 6291464 | tf_op jit(solution)/shard_map/ppermute | solution.py:240
  14.4 8.0 %all-to-all-start = ((s32[8,8,128]{2,1,0:T(8,128)}), s32[8,8,128]{2,1,0:T(8,128)S(1)}, u32[]{:S(2)}, u32[]{:S(2)}) async-start(s32[8,8,128]{2,1,0:T(8,128)} %shard_map.93), calls=%async_computation | async-start | bytes 65536 | tf_op jit(solution)/shard_map/all_to_all | solution.py:236
  22.4 1.6 %copy-start.2 = (bf16[1024,1024]{1,0:T(8,128)(2,1)S(1)}, bf16[1024,1024]{1,0:T(8,128)(2,1)}, u32[]{:S(2)}) copy-start(bf16[1024,1024]{1,0:T(8,128)(2,1)} %mine.1) | copy-start | bytes 6291460
  53.4 23.0 %all-to-all-start.3 = ((f32[12,40,128]{2,1,0:T(8,128)}), f32[12,40,128]{2,1,0:T(8,128)S(1)}, u32[]{:S(2)}, u32[]{:S(2)}) async-start(f32[12,40,128]{2,1,0:T(8,128)} %shard_map.97), calls=%async_computation.3 | async-start | bytes 491520 | tf_op jit(solution)/shard_map/all_to_all | solution.py:236
  64.7 16.4 %collective-permute-start.1 = (bf16[2,128,1024]{2,1,0:T(8,128)(2,1)}, bf16[2,128,1024]{2,1,0:T(8,128)(2,1)S(1)}, u32[]{:S(2)}, u32[]{:S(2)}) collective-permute-start(bf16[2,128,1024]{2,1,0:T(8,128)(2,1)} %get-tuple-element.14), channel_id=1, source_target_pairs={{0,2},{2,4},{4,6},{6,0},{1,3},{3,5},{5,7},{7,1},{8,10},{10,12},{12... | collective-permute-start | bytes 1572872 | tf_op jit(solution)/shard_map/ppermute | solution.py:295
  66.9 21.7 %collective-permute-start.2 = (bf16[2,128,1024]{2,1,0:T(8,128)(2,1)S(1)}, bf16[2,128,1024]{2,1,0:T(8,128)(2,1)S(1)}, u32[]{:S(2)}, u32[]{:S(2)}) collective-permute-start(bf16[2,128,1024]{2,1,0:T(8,128)(2,1)S(1)} %get-tuple-element.15), channel_id=1, source_target_pairs={{0,4},{2,6},{4,0},{6,2},{1,5},{3,7},{5,1},{7,3},{8,12},{10,14},{12... | collective-permute-start | bytes 1572872 | tf_op jit(solution)/shard_map/ppermute | solution.py:295
  70.6 23.8 %collective-permute-start.3 = (bf16[2,128,1024]{2,1,0:T(8,128)(2,1)S(1)}, bf16[2,128,1024]{2,1,0:T(8,128)(2,1)S(1)}, u32[]{:S(2)}, u32[]{:S(2)}) collective-permute-start(bf16[2,128,1024]{2,1,0:T(8,128)(2,1)S(1)} %get-tuple-element.16), channel_id=1, source_target_pairs={{0,6},{2,0},{4,2},{6,4},{1,7},{3,1},{5,3},{7,5},{8,14},{10,8},{12,... | collective-permute-start | bytes 1572872 | tf_op jit(solution)/shard_map/ppermute | solution.py:295
  77.7 16.6 %all-to-all-start.4 = ((f32[8,32,128]{2,1,0:T(8,128)}), f32[8,32,128]{2,1,0:T(8,128)S(1)}, u32[]{:S(2)}, u32[]{:S(2)}) async-start(f32[8,32,128]{2,1,0:T(8,128)} %shard_map.98), calls=%async_computation.4 | async-start | bytes 262144 | tf_op jit(solution)/shard_map/all_to_all | solution.py:236
  94.9 18.7 %copy-start = (s32[256]{0:T(256)S(1)}, s32[256]{0:T(256)}, u32[]{:S(2)}) copy-start(s32[256]{0:T(256)} %param.10) | copy-start | bytes 3076
  95.0 18.7 %copy-start.1 = (s32[32]{0:T(128)S(1)}, s32[32]{0:T(128)}, u32[]{:S(2)}) copy-start(s32[32]{0:T(128)} %param.11) | copy-start | bytes 388
  107.9 5.7 %collective-permute-start.4 = (f32[4,256,128]{2,1,0:T(8,128)S(1)}, f32[4,256,128]{2,1,0:T(8,128)S(1)}, u32[]{:S(2)}, u32[]{:S(2)}) collective-permute-start(f32[4,256,128]{2,1,0:T(8,128)S(1)} %all_to_all.32.kept), channel_id=1, source_target_pairs={{0,1},{1,0},{2,3},{3,2},{4,5},{5,4},{6,7},{7,6},{8,9},{9,8},{10,11... | collective-permute-start | bytes 1572872 | tf_op jit(solution)/shard_map/ppermute | solution.py:240

commit v4 on v3

--- a/solution.py
+++ b/solution.py
@@ -89,8 +89,14 @@
     return total
 
 
-def main_kernel(pos, known, mine, theirs, out, child, *refs):
-    sent, (weights, sems) = refs[:-2], refs[-2:]
+def main_kernel(pos, known, mine_far, theirs_far, out, child, *refs):
+    sent, (weights, mine, theirs, loads, sems) = refs[:-5], refs[-5:]
+    fetches = [
+        pltpu.make_async_copy(source, target, loads.at[i])
+        for i, (source, target) in enumerate([(mine_far, mine), (theirs_far, theirs)])
+    ]
+    for fetch in fetches:
+        fetch.start()
     groups, kdev = known.shape[0], known.shape[2]
     nx, height, lanes = out.shape
     half = weights.shape[1] // 3
@@ -103,8 +109,6 @@
             copies.append(
                 pltpu.make_async_copy(rows.at[at, :], target.at[which], sems.at[k, which])
             )
-    for copy in copies:
-        copy.start()
     ks = iota((kdev, LANES), 0) + 1
     k2s = iota((half, kdev), 0) + c * half
     diagonal = iota((kdev, LANES), 0) == iota((kdev, LANES), 1)
@@ -124,12 +128,20 @@
             ids = known[2 * x + core, b : b + 1, :] & 255
             onehot = jnp.where(ids == ks, 1.0, 0.0).astype(BF16)
             weights[which, :, b * kdev : (b + 1) * kdev] = dot(parts, onehot).astype(BF16)
-    for j in range(nx):
-        at = slice(j * 2 * lanes, (j + 1) * 2 * lanes)
-        total = dot(weights[0], mine[:, at]) + dot(weights[1], theirs[:, at])
-        total = total[:half] + total[half : 2 * half] + total[2 * half :]
-        out[j, :half] = total[:, :lanes]
-        out[j, half:] = total[:, lanes:]
+    for which, rows in enumerate((mine, theirs)):
+        fetches[which].wait()
+        for copy in copies[which::2]:
+            copy.start()
+        for j in range(nx):
+            at = slice(j * 2 * lanes, (j + 1) * 2 * lanes)
+            total = dot(weights[which], rows[:, at])
+            total = total[:half] + total[half : 2 * half] + total[2 * half :]
+            if which == 0:
+                out[j, :half] = total[:, :lanes]
+                out[j, half:] = total[:, lanes:]
+            else:
+                out[j, :half] = out[j, :half] + total[:, :lanes]
+                out[j, half:] = out[j, half:] + total[:, lanes:]
     counts = replicated_count(children)
     ny = child.shape[0]
     rows = half // ny
@@ -272,15 +284,19 @@
         main_kernel,
         pos,
         (known, points, theirs),
-        [whole((groups, groups, cap)), whole((slots, depth)), whole((slots, depth))],
+        [whole((groups, groups, cap))] + [pl.BlockSpec(memory_space=pltpu.HBM)] * 2,
         [shape((nx, 2 * half, LANES), F32), shape((ny, 8, LANES), F32)]
         + [shape((nc, cap, depth), BF16)] * nx,
         flops=2 * 6 * slots * half * depth,
         scratch=[
             pltpu.VMEM((nc, 3 * half, slots), BF16),
+            pltpu.VMEM((slots, depth), BF16),
+            pltpu.VMEM((slots, depth), BF16),
+            pltpu.SemaphoreType.DMA((2,)),
             pltpu.SemaphoreType.DMA((nx, nc)),
         ],
         far=nx,
+        limit=24,
     )
     partial = exchange(partial, "x")
 

time: 116 us -> 116 us (level)
  no operation moved by 1% of the time
where the time goes in v4:
time: 116 us; the launch traced here: 115 us
  starting transfers between devices  42.7 us (37%)
  blocking collectives  34.6 us (30%)
  waiting for transfers between devices  21.1 us (18%)
  Pallas kernels  14.1 us (12%)
  local copies, waits for them, and re-layouts  1.6 us (1%)
    all_to_all x3, blocking collectives, exchange(): return lax.all_to_all(rows, axes, split_axis=0, concat_axis=0, tiled=True)  34.6 us
    all_to_all x3, starting transfers between devices, exchange(): return lax.all_to_all(rows, axes, split_axis=0, concat_axis=0, tiled=True)  18 us
    ppermute x2, starting transfers between devices, swap(): return lax.ppermute(rows, 'c', [(0, 1), (1, 0)])  16.3 us
    ppermute x3, waiting for transfers between devices, local(): lax.ppermute(v, 'x', [(j, (j + k) % nx) for j in range(nx)])  13.3 us
    pallas_call x7, Pallas kernels, call(): pl.pallas_call(body, grid_spec=pltpu.PrefetchScalarGridSpec(num_scalar_pr...  12.7 us
    ppermute x3, starting transfers between devices, local(): lax.ppermute(v, 'x', [(j, (j + k) % nx) for j in range(nx)])  8.43 us
    all_to_all x3, waiting for transfers between devices, exchange(): return lax.all_to_all(rows, axes, split_axis=0, concat_axis=0, tiled=True)  7.89 us
  transfers between devices with their start and end apart: 8, of which 4 were waited for; matrix products, arithmetic and copies ran while one was open for 0% of the time, Pallas kernels for 4%

profile of v4, /device:TPU:1, one launch (start us, length us, event | category | flops | bytes accessed | tf_op | source)
XLA Modules:
  0.0 114.9 jit_solution(12210002872312877463)
XLA Ops:
  0.6 12.4 %collective-permute-start = (bf16[1024,1024]{1,0:T(8,128)(2,1)}, bf16[1024,1024]{1,0:T(8,128)(2,1)}, u32[]{:S(2)}, u32[]{:S(2)}) collective-permute-start(bf16[1024,1024]{1,0:T(8,128)(2,1)} %mine_far.1), channel_id=1, source_target_pairs={{0,1},{1,0},{2,3},{3,2},{4,5},{5,4},{6,7},{7,6},{8,9},{9,8},{10,11... | collective-permute-start | bytes 6291464 | tf_op jit(solution)/shard_map/ppermute | solution.py:252
  13.1 1.3 %shard_map.93 = s32[8,8,128]{2,1,0:T(8,128)} custom-call(s32[1,8]{1,0:T(1,128)} %live.1, s32[8,128]{1,0:T(8,128)} %bitcast.8, s32[1,128]{1,0:T(1,128)} %bitcast.9), custom_call_target="tpu_custom_call" | custom-call | tf_op jit(solution)/shard_map/pallas_call | solution.py:267
  14.4 3.3 %all-to-all-start = ((s32[8,8,128]{2,1,0:T(8,128)}), s32[8,8,128]{2,1,0:T(8,128)S(1)}, u32[]{:S(2)}, u32[]{:S(2)}) async-start(s32[8,8,128]{2,1,0:T(8,128)} %shard_map.93), calls=%async_computation | async-start | bytes 65536 | tf_op jit(solution)/shard_map/all_to_all | solution.py:248
  17.7 0.1 pad_add_fusion.pos
  17.8 4.6 %all-to-all-done.known = s32[8,8,128]{2,1,0:T(8,128)S(1)} async-done(((s32[8,8,128]{2,1,0:T(8,128)}), s32[8,8,128]{2,1,0:T(8,128)S(1)}, u32[]{:S(2)}, u32[]{:S(2)}) %all-to-all-start) | async-done | bytes 32800 | tf_op jit(solution)/shard_map/all_to_all | solution.py:248
  22.4 0.0 collective-permute-done.theirs_far
  22.4 0.0 copy-start.2
  22.4 1.6 %copy-done.2 = bf16[1024,1024]{1,0:T(8,128)(2,1)S(1)} copy-done((bf16[1024,1024]{1,0:T(8,128)(2,1)S(1)}, bf16[1024,1024]{1,0:T(8,128)(2,1)}, u32[]{:S(2)}) %copy-start.2) | copy-done | bytes 2097176
  24.0 5.1 %shard_map.94 = (f32[4,256,128]{2,1,0:T(8,128)S(1)}, f32[8,8,128]{2,1,0:T(8,128)S(1)}, bf16[2,128,1024]{2,1,0:T(8,128)(2,1)S(1)}, bf16[2,128,1024]{2,1,0:T(8,128...) custom-call(s32[2]{0:T(128)S(1)} %pad_add_fusion.pos, s32[8,8,128]{2,1,0:T(8,128)S(1)} %all-to-all-done.known, ...), custom_call_target="tpu_custom_call" | custom-call | flops 1610612736 | bytes 6881280 | tf_op jit(solution)/shard_map/pallas_call | solution.py:39
  29.1 10.9 %all_to_all.30.parts = f32[4,256,128]{2,1,0:T(8,128)S(1)} all-to-all(f32[4,256,128]{2,1,0:T(8,128)S(1)} %get-tuple-element.17), channel_id=1, replica_groups=mesh['y'=8,'z'=12,'x'=4,'c'=2] {'x'}, dimensions={0} | all-to-all | bytes 1048576 | tf_op jit(solution)/shard_map/all_to_all | solution.py:248
  40.0 0.6 shard_map.96
  40.6 10.7 %all_to_all.31.parts = f32[8,40,128]{2,1,0:T(8,128)S(1)} all-to-all(f32[8,40,128]{2,1,0:T(8,128)S(1)} %shard_map.96), channel_id=1, replica_groups=mesh['y'=8,'z'=12,'x'=4,'c'=2] {'y'}, dimensions={0} | all-to-all | bytes 327680 | tf_op jit(solution)/shard_map/all_to_all | solution.py:248
  51.3 1.3 %shard_map.97 = f32[12,40,128]{2,1,0:T(8,128)} custom-call(s32[2]{0:T(128)S(1)} %pad_add_fusion.pos, f32[8,40,128]{2,1,0:T(8,128)S(1)} %all_to_all.31.parts), custom_call_target="tpu_custom_call" | custom-call | bytes 409600 | tf_op jit(solution)/shard_map/pallas_call | solution.py:39
  52.6 11.3 %all-to-all-start.3 = ((f32[12,40,128]{2,1,0:T(8,128)}), f32[12,40,128]{2,1,0:T(8,128)S(1)}, u32[]{:S(2)}, u32[]{:S(2)}) async-start(f32[12,40,128]{2,1,0:T(8,128)} %shard_map.97), calls=%async_computation.3 | async-start | bytes 491520 | tf_op jit(solution)/shard_map/all_to_all | solution.py:248
  63.9 2.2 %collective-permute-start.1 = (bf16[2,128,1024]{2,1,0:T(8,128)(2,1)}, bf16[2,128,1024]{2,1,0:T(8,128)(2,1)S(1)}, u32[]{:S(2)}, u32[]{:S(2)}) collective-permute-start(bf16[2,128,1024]{2,1,0:T(8,128)(2,1)} %get-tuple-element.14), channel_id=1, source_target_pairs={{0,2},{2,4},{4,6},{6,0},{1,3},{3,5},{5,7},{7,1},{8,10},{10,12},{12... | collective-permute-start | bytes 1572872 | tf_op jit(solution)/shard_map/ppermute | solution.py:311
  66.1 3.7 %collective-permute-start.2 = (bf16[2,128,1024]{2,1,0:T(8,128)(2,1)S(1)}, bf16[2,128,1024]{2,1,0:T(8,128)(2,1)S(1)}, u32[]{:S(2)}, u32[]{:S(2)}) collective-permute-start(bf16[2,128,1024]{2,1,0:T(8,128)(2,1)S(1)} %get-tuple-element.15), channel_id=1, source_target_pairs={{0,4},{2,6},{4,0},{6,2},{1,5},{3,7},{5,1},{7,3},{8,12},{10,14},{12... | collective-permute-start | bytes 1572872 | tf_op jit(solution)/shard_map/ppermute | solution.py:311
  69.8 2.6 %collective-permute-start.3 = (bf16[2,128,1024]{2,1,0:T(8,128)(2,1)S(1)}, bf16[2,128,1024]{2,1,0:T(8,128)(2,1)S(1)}, u32[]{:S(2)}, u32[]{:S(2)}) collective-permute-start(bf16[2,128,1024]{2,1,0:T(8,128)(2,1)S(1)} %get-tuple-element.16), channel_id=1, source_target_pairs={{0,6},{2,0},{4,2},{6,4},{1,7},{3,1},{5,3},{7,5},{8,14},{10,8},{12,... | collective-permute-start | bytes 1572872 | tf_op jit(solution)/shard_map/ppermute | solution.py:311
  72.3 3.3 %all-to-all-done.3.parts = f32[12,40,128]{2,1,0:T(8,128)S(1)} async-done(((f32[12,40,128]{2,1,0:T(8,128)}), f32[12,40,128]{2,1,0:T(8,128)S(1)}, u32[]{:S(2)}, u32[]{:S(2)}) %all-to-all-start.3) | async-done | bytes 245792 | tf_op jit(solution)/shard_map/all_to_all | solution.py:248
  75.6 1.3 %shard_map.98 = f32[8,32,128]{2,1,0:T(8,128)} custom-call(s32[2]{0:T(128)S(1)} %pad_add_fusion.pos, f32[12,40,128]{2,1,0:T(8,128)S(1)} %all-to-all-done.3.parts), custom_call_target="tpu_custom_call" | custom-call | bytes 376832 | tf_op jit(solution)/shard_map/pallas_call | solution.py:39
  76.9 3.4 %all-to-all-start.4 = ((f32[8,32,128]{2,1,0:T(8,128)}), f32[8,32,128]{2,1,0:T(8,128)S(1)}, u32[]{:S(2)}, u32[]{:S(2)}) async-start(f32[8,32,128]{2,1,0:T(8,128)} %shard_map.98), calls=%async_computation.4 | async-start | bytes 262144 | tf_op jit(solution)/shard_map/all_to_all | solution.py:248
  80.3 0.0 collective-permute-done.1.refs_1_.refs_0_
  80.3 7.5 %collective-permute-done.2.refs_2_.refs_1_ = bf16[2,128,1024]{2,1,0:T(8,128)(2,1)S(1)} collective-permute-done((bf16[2,128,1024]{2,1,0:T(8,128)(2,1)S(1)}, bf16[2,128,1024]{2,1,0:T(8,128)(2,1)S(1)}, u32[]{:S(2)}, u32[]{:S(2)}) %collective-permute-start.2) | collective-permute-done | bytes 524320 | tf_op jit(solution)/shard_map/ppermute | solution.py:311
  87.8 5.8 %collective-permute-done.3.refs_3_.refs_2_ = bf16[2,128,1024]{2,1,0:T(8,128)(2,1)S(1)} collective-permute-done((bf16[2,128,1024]{2,1,0:T(8,128)(2,1)S(1)}, bf16[2,128,1024]{2,1,0:T(8,128)(2,1)S(1)}, u32[]{:S(2)}, u32[]{:S(2)}) %collective-permute-start.3) | collective-permute-done | bytes 524320 | tf_op jit(solution)/shard_map/ppermute | solution.py:311
  93.5 0.0 all-to-all-done.4.two
  93.6 0.6 shard_map.99
  94.1 0.0 copy-start
  94.1 0.0 copy-start.1
  94.2 13.0 %all_to_all.32.kept = f32[4,256,128]{2,1,0:T(8,128)S(1)} all-to-all(f32[4,256,128]{2,1,0:T(8,128)S(1)} %shard_map.99), channel_id=1, replica_groups=mesh['y'=8,'z'=12,'x'=4,'c'=2] {'x'}, dimensions={0} | all-to-all | bytes 1048576 | tf_op jit(solution)/shard_map/all_to_all | solution.py:248
  107.1 3.8 %collective-permute-start.4 = (f32[4,256,128]{2,1,0:T(8,128)S(1)}, f32[4,256,128]{2,1,0:T(8,128)S(1)}, u32[]{:S(2)}, u32[]{:S(2)}) collective-permute-start(f32[4,256,128]{2,1,0:T(8,128)S(1)} %all_to_all.32.kept), channel_id=1, source_target_pairs={{0,1},{1,0},{2,3},{3,2},{4,5},{5,4},{6,7},{7,6},{8,9},{9,8},{10,11... | collective-permute-start | bytes 1572872 | tf_op jit(solution)/shard_map/ppermute | solution.py:252
  111.0 1.8 %shard_map.95 = f32[128,1024]{1,0:T(8,128)} custom-call(s32[2]{0:T(128)S(1)} %pad_add_fusion.pos, s32[8,8,128]{2,1,0:T(8,128)S(1)} %all-to-all-done.known, bf16[2,128,1024]{2,1,0:T(8,128)(2,1)S(1)} %get-tuple-element.13.refs_0_, bf16[2,128,1024]{2,1,0:T(8,128)(2,1)S(1)} %collective-permute-done.1.refs_1_.refs_0_, ...), custom_call_target="tpu_custom_call" | custom-call | flops 268435456 | bytes 2654208 | tf_op jit(solution)/shard_map/pallas_call | solution.py:39
  112.8 0.0 collective-permute-done.4.got
  112.8 0.0 copy-done
  112.8 0.0 copy-done.1
  112.8 2.1 %shard_map.100 = (f32[256,1024]{1,0:T(8,128)}, f32[32,1024]{1,0:T(8,128)}, f32[8,1024]{1,0:T(8,128)}) custom-call(s32[2]{0:T(128)S(1)} %pad_add_fusion.pos, f32[4,256,128]{2,1,0:T(8,128)S(1)} %all_to_all.32.kept, f32[4,256,128]{2,1,0:T(8,128)S(1)} %collective-permute-done.4.got, s32[1,256]{1,0:T(1,128)S(1)} %bitcast.6, s32[1,32]{1,0:T(1,128)S(1)} %bitcast.7), custom_call_target="tpu_custom_call" | custom-call | bytes 2262144 | tf_op jit(solution)/shard_map/pallas_call | solution.py:39
Async XLA Ops:
  0.6 21.8 %collective-permute-start = (bf16[1024,1024]{1,0:T(8,128)(2,1)}, bf16[1024,1024]{1,0:T(8,128)(2,1)}, u32[]{:S(2)}, u32[]{:S(2)}) collective-permute-start(bf16[1024,1024]{1,0:T(8,128)(2,1)} %mine_far.1), channel_id=1, source_target_pairs={{0,1},{1,0},{2,3},{3,2},{4,5},{5,4},{6,7},{7,6},{8,9},{9,8},{10,11... | collective-permute-start | bytes 6291464 | tf_op jit(solution)/shard_map/ppermute | solution.py:252
  14.4 8.0 %all-to-all-start = ((s32[8,8,128]{2,1,0:T(8,128)}), s32[8,8,128]{2,1,0:T(8,128)S(1)}, u32[]{:S(2)}, u32[]{:S(2)}) async-start(s32[8,8,128]{2,1,0:T(8,128)} %shard_map.93), calls=%async_computation | async-start | bytes 65536 | tf_op jit(solution)/shard_map/all_to_all | solution.py:248
  22.4 1.6 %copy-start.2 = (bf16[1024,1024]{1,0:T(8,128)(2,1)S(1)}, bf16[1024,1024]{1,0:T(8,128)(2,1)}, u32[]{:S(2)}) copy-start(bf16[1024,1024]{1,0:T(8,128)(2,1)} %mine_far.1) | copy-start | bytes 6291460
  52.6 23.0 %all-to-all-start.3 = ((f32[12,40,128]{2,1,0:T(8,128)}), f32[12,40,128]{2,1,0:T(8,128)S(1)}, u32[]{:S(2)}, u32[]{:S(2)}) async-start(f32[12,40,128]{2,1,0:T(8,128)} %shard_map.97), calls=%async_computation.3 | async-start | bytes 491520 | tf_op jit(solution)/shard_map/all_to_all | solution.py:248
  63.9 16.4 %collective-permute-start.1 = (bf16[2,128,1024]{2,1,0:T(8,128)(2,1)}, bf16[2,128,1024]{2,1,0:T(8,128)(2,1)S(1)}, u32[]{:S(2)}, u32[]{:S(2)}) collective-permute-start(bf16[2,128,1024]{2,1,0:T(8,128)(2,1)} %get-tuple-element.14), channel_id=1, source_target_pairs={{0,2},{2,4},{4,6},{6,0},{1,3},{3,5},{5,7},{7,1},{8,10},{10,12},{12... | collective-permute-start | bytes 1572872 | tf_op jit(solution)/shard_map/ppermute | solution.py:311
  66.1 21.7 %collective-permute-start.2 = (bf16[2,128,1024]{2,1,0:T(8,128)(2,1)S(1)}, bf16[2,128,1024]{2,1,0:T(8,128)(2,1)S(1)}, u32[]{:S(2)}, u32[]{:S(2)}) collective-permute-start(bf16[2,128,1024]{2,1,0:T(8,128)(2,1)S(1)} %get-tuple-element.15), channel_id=1, source_target_pairs={{0,4},{2,6},{4,0},{6,2},{1,5},{3,7},{5,1},{7,3},{8,12},{10,14},{12... | collective-permute-start | bytes 1572872 | tf_op jit(solution)/shard_map/ppermute | solution.py:311
  69.8 23.8 %collective-permute-start.3 = (bf16[2,128,1024]{2,1,0:T(8,128)(2,1)S(1)}, bf16[2,128,1024]{2,1,0:T(8,128)(2,1)S(1)}, u32[]{:S(2)}, u32[]{:S(2)}) collective-permute-start(bf16[2,128,1024]{2,1,0:T(8,128)(2,1)S(1)} %get-tuple-element.16), channel_id=1, source_target_pairs={{0,6},{2,0},{4,2},{6,4},{1,7},{3,1},{5,3},{7,5},{8,14},{10,8},{12,... | collective-permute-start | bytes 1572872 | tf_op jit(solution)/shard_map/ppermute | solution.py:311
  76.9 16.6 %all-to-all-start.4 = ((f32[8,32,128]{2,1,0:T(8,128)}), f32[8,32,128]{2,1,0:T(8,128)S(1)}, u32[]{:S(2)}, u32[]{:S(2)}) async-start(f32[8,32,128]{2,1,0:T(8,128)} %shard_map.98), calls=%async_computation.4 | async-start | bytes 262144 | tf_op jit(solution)/shard_map/all_to_all | solution.py:248
  94.1 18.7 %copy-start = (s32[256]{0:T(256)S(1)}, s32[256]{0:T(256)}, u32[]{:S(2)}) copy-start(s32[256]{0:T(256)} %param.10) | copy-start | bytes 3076
  94.1 18.7 %copy-start.1 = (s32[32]{0:T(128)S(1)}, s32[32]{0:T(128)}, u32[]{:S(2)}) copy-start(s32[32]{0:T(128)} %param.11) | copy-start | bytes 388
  107.1 5.7 %collective-permute-start.4 = (f32[4,256,128]{2,1,0:T(8,128)S(1)}, f32[4,256,128]{2,1,0:T(8,128)S(1)}, u32[]{:S(2)}, u32[]{:S(2)}) collective-permute-start(f32[4,256,128]{2,1,0:T(8,128)S(1)} %all_to_all.32.kept), channel_id=1, source_target_pairs={{0,1},{1,0},{2,3},{3,2},{4,5},{5,4},{6,7},{7,6},{8,9},{9,8},{10,11... | collective-permute-start | bytes 1572872 | tf_op jit(solution)/shard_map/ppermute | solution.py:252
